TPU v7x, 32 devices: a whole 2x2x4 slice. The times are simulated.
32 devices in a mesh: groups: 2 (over y), patch: 4 (over z), chan: 2 (over x), sub: 2 (over core).
Axes of the slice: x: 2, y: 2, z: 4, core: 2. Of those that a mesh axis runs over, the one named last changes fastest.
Arguments:
- latent: bfloat16 [640, 2048], P(('chan', 'sub'), ('groups', 'patch')), parts along dimension 1, may hold values from -18 to 18
- timestep: int32 [2], P('groups'), parts along dimension 0, may hold values from 0 to 999
- time_w1: bfloat16 [1280, 320], replicated, may hold values from -0.3125 to 0.3125
- time_proj: bfloat16 [640, 1280], P(('chan', 'sub')), may hold values from -0.15625 to 0.15625
- conv1_w: bfloat16 [9, 640, 640], P(None, ('chan', 'sub')), may hold values from -0.078125 to 0.078125
- conv2_w: bfloat16 [9, 640, 640], P(None, ('chan', 'sub')), may hold values from -0.078125 to 0.078125
- proj_in_w: bfloat16 [640, 640], P(('chan', 'sub')), may hold values from -0.25 to 0.25
- q_w: bfloat16 [640, 640], P(('chan', 'sub')), may hold values from -8 to 8
- kv_w: bfloat16 [2, 640, 640], P(None, ('chan', 'sub')), may hold values from -8 to 8
- out_w: bfloat16 [640, 640], P(('chan', 'sub')), may hold values from -0.25 to 0.25
- proj_out_w: bfloat16 [640, 640], P(('chan', 'sub')), may hold values from -0.25 to 0.25
Outputs:
- output: bfloat16 [640, 2048], P(('chan', 'sub'), ('groups', 'patch')), parts along dimension 1
There are 2 independent parts, one for each index of `groups`. A program takes and returns all parts, laid end to end along the dimension named above; an argument that names none is the same for every part. Nothing has to cross between parts.
All inputs are finite; a program needn't handle non-finite values.
Results may differ from a plain program's by a relative error of at most 0.02.
Values may be sent and summed in bfloat16 or wider, within the bound.
A program may use at most 64 MiB of HBM per device.

v0:
```python
import math

import jax
import jax.numpy as jnp
from jax import lax
from jax.sharding import PartitionSpec as P

C = 640
HEADS = 10
HEAD_DIM = 64
NGROUPS = 32
FREQ = 320
WIDTH = 256


def with_halo(cells, sides, width):
    for axis, dim in sides:
        count = lax.axis_size(axis)
        ends = count - 1
        head = lax.slice_in_dim(cells, 0, width, axis=dim)
        tail = lax.slice_in_dim(cells, cells.shape[dim] - width, cells.shape[dim], axis=dim)
        cells = jnp.concatenate(
            [
                lax.ppermute(tail, axis, [(i, (i + 1) % count) for i in range(ends)]),
                cells,
                lax.ppermute(head, axis, [((i + 1) % count, i) for i in range(ends)]),
            ],
            axis=dim,
        )
    return cells


def from_behind(array, axis, by):
    count = lax.axis_size(axis)
    return lax.ppermute(array, axis, [(i, (i + by) % count) for i in range(count)])


def merged(array, axis, combine):
    everything = jax.tree.map(lambda part: lax.all_gather(part, axis), array)
    first = jax.tree.map(lambda part: part[0], everything)

    def turn(k, so_far):
        return combine(so_far, jax.tree.map(lambda part: part[k], everything))

    return lax.fori_loop(1, lax.axis_size(axis), turn, first)


def group_norm(values, epsilon):
    channels, band_len = values.shape
    group_size = C // NGROUPS
    grouped = values.reshape(channels // group_size, group_size, band_len)
    cell_count = group_size * band_len * lax.axis_size("patch")
    centre = lax.psum(jnp.sum(grouped, axis=(1, 2)), "patch") / cell_count
    shifted = grouped - centre[:, None, None]
    spread = lax.psum(jnp.sum(shifted * shifted, axis=(1, 2)), "patch") / cell_count
    normal_form = (grouped - centre[:, None, None]) * lax.rsqrt(spread + epsilon)[:, None, None]
    return normal_form.reshape(channels, band_len)


def convolve(active, weight):
    own_channels, band_len = active.shape
    height = band_len // WIDTH
    whole_rows = lax.all_gather(active, ("chan", "sub"), axis=0, tiled=True)
    image_grid = whole_rows.reshape(whole_rows.shape[0], height, WIDTH)
    padded = with_halo(image_grid, (("patch", 1),), 1)
    channels = padded.shape[0]
    padded = jnp.pad(padded, ((0, 0), (0, 0), (1, 1)))
    running = jnp.zeros((weight.shape[1], band_len), jnp.float32)
    for offset in range(9):
        row_step, col_step = divmod(offset, 3)
        window = padded[:, row_step : row_step + height, col_step : col_step + WIDTH].reshape(
            channels, band_len
        )
        running = running + jnp.dot(weight[offset], window, preferred_element_type=jnp.float32)
    return running


def combine_parts(earlier_part, later_part):
    peak_one, total_one, sums_one = earlier_part
    peak_two, total_two, sums_two = later_part
    new_peak = jnp.maximum(peak_one, peak_two)
    factor_one = jnp.exp(peak_one - new_peak)
    factor_two = jnp.exp(peak_two - new_peak)
    new_total = total_one * factor_one + total_two * factor_two
    new_sums = sums_one * factor_one[:, None, :] + sums_two * factor_two[:, None, :]
    return (new_peak, new_total, new_sums)


def advance(kv_piece):
    return from_behind(kv_piece, "patch", 1)


def local(
    latent, timestep, time_w1, time_proj, conv1_w, conv2_w, proj_in_w, q_w, kv_w, out_w, proj_out_w
):
    latent_f32 = latent.astype(jnp.float32)
    band_len = latent.shape[1]
    half_width = FREQ // 2
    frequency = jnp.exp(-math.log(10000.0) * jnp.arange(half_width, dtype=jnp.float32) / half_width)
    angles = timestep[0].astype(jnp.float32) * frequency
    embedded = jnp.concatenate([jnp.cos(angles), jnp.sin(angles)]).astype(jnp.bfloat16)
    time_hidden = jax.nn.silu(jnp.dot(time_w1, embedded, preferred_element_type=jnp.float32))
    time_bias = jnp.dot(
        time_proj, jax.nn.silu(time_hidden).astype(jnp.bfloat16), preferred_element_type=jnp.float32
    )
    act_one = jax.nn.silu(group_norm(latent_f32, 1e-05)).astype(jnp.bfloat16)
    conv_one = (convolve(act_one, conv1_w) + time_bias[:, None]).astype(jnp.bfloat16)
    act_two = jax.nn.silu(group_norm(conv_one.astype(jnp.float32), 1e-05)).astype(jnp.bfloat16)
    resnet = (latent_f32 + convolve(act_two, conv2_w)).astype(jnp.bfloat16)
    normed = group_norm(resnet.astype(jnp.float32), 1e-06).astype(jnp.bfloat16)
    columns = proj_in_w
    projected = jnp.dot(
        columns,
        lax.all_gather(normed, ("chan", "sub"), axis=0, tiled=True),
        preferred_element_type=jnp.float32,
    ).astype(jnp.bfloat16)
    whole_proj = lax.all_gather(projected, ("chan", "sub"), axis=0, tiled=True).astype(jnp.float32)
    centre = jnp.mean(whole_proj, axis=0, keepdims=True)
    spread = jnp.mean((whole_proj - centre) * (whole_proj - centre), axis=0, keepdims=True)
    layer_normed = ((whole_proj - centre) / jnp.sqrt(spread + 1e-05)).astype(jnp.bfloat16)
    query_own = (jnp.dot(q_w, layer_normed, preferred_element_type=jnp.float32) * 0.125).astype(
        jnp.bfloat16
    )
    queries = lax.all_gather(query_own, ("chan", "sub"), axis=0, tiled=True).reshape(
        HEADS, HEAD_DIM, band_len
    )
    key_value = jnp.einsum(
        "joc,cb->jbo", kv_w, layer_normed, preferred_element_type=jnp.float32
    ).astype(jnp.bfloat16)
    slot_pairs = lax.all_to_all(key_value, ("chan", "sub"), split_axis=1, concat_axis=2, tiled=True)

    def attend(softmax_state, kv_piece):
        row_peak, row_total, weighted = softmax_state
        slot_len = kv_piece.shape[1]
        key_heads = kv_piece[0].reshape(slot_len, HEADS, HEAD_DIM)
        value_heads = kv_piece[1].reshape(slot_len, HEADS, HEAD_DIM)
        scores = jnp.einsum("khd,hdb->hkb", key_heads, queries, preferred_element_type=jnp.float32)
        new_peak = jnp.maximum(row_peak, jnp.max(scores, axis=1))
        factor = jnp.exp(row_peak - new_peak)
        weights = jnp.exp(scores - new_peak[:, None, :])
        new_total = row_total * factor + jnp.sum(weights, axis=1)
        update = jnp.einsum(
            "khd,hkb->hdb",
            value_heads,
            weights.astype(jnp.bfloat16),
            preferred_element_type=jnp.float32,
        )
        return (new_peak, new_total, weighted * factor[:, None, :] + update)

    start_state = (
        jnp.full((HEADS, band_len), -1e30, jnp.float32),
        jnp.zeros((HEADS, band_len), jnp.float32),
        jnp.zeros((HEADS, HEAD_DIM, band_len), jnp.float32),
    )
    softmax_state = attend(start_state, slot_pairs)
    band_count = lax.axis_size("patch")

    def one_side(step_index, packed):
        state_now, ahead = packed
        ahead = advance(ahead)
        return (attend(state_now, ahead), ahead)

    softmax_state, ahead = lax.fori_loop(0, band_count - 1, one_side, (softmax_state, slot_pairs))
    row_peak, row_total, weighted = merged(softmax_state, ("chan", "sub"), combine_parts)
    attended = (
        (weighted / row_total[:, None, :]).reshape(HEADS * HEAD_DIM, band_len).astype(jnp.bfloat16)
    )
    mixed = (
        projected.astype(jnp.float32) + jnp.dot(out_w, attended, preferred_element_type=jnp.float32)
    ).astype(jnp.bfloat16)
    columns = proj_out_w
    final_sum = resnet.astype(jnp.float32) + jnp.dot(
        columns,
        lax.all_gather(mixed, ("chan", "sub"), axis=0, tiled=True),
        preferred_element_type=jnp.float32,
    )
    return final_sum.astype(jnp.bfloat16)


def solution(mesh):
    in_specs = (
        P(("chan", "sub"), ("groups", "patch")),
        P("groups"),
        P(),
        P(("chan", "sub"), None),
        P(None, ("chan", "sub"), None),
        P(None, ("chan", "sub"), None),
        P(("chan", "sub"), None),
        P(("chan", "sub"), None),
        P(None, ("chan", "sub"), None),
        P(("chan", "sub"), None),
        P(("chan", "sub"), None),
    )
    out_specs = P(("chan", "sub"), ("groups", "patch"))
    return jax.shard_map(local, mesh=mesh, in_specs=in_specs, out_specs=out_specs, check_vma=False)
```

profile of v0, /device:TPU:1, one launch (start us, length us, event | category | flops | bytes accessed | tf_op | source)
XLA Modules:
  0.0 231.2 jit_solution(6947389749806903160)
XLA Ops:
  7.9 10.8 %psum.42 = f32[8]{0:T(128)S(1)} all-reduce(f32[8]{0:T(128)S(1)} %reduce_sum.106), channel_id=1, replica_groups=mesh['groups'=2,'patch'=4,'chan'=2,'sub'=2] {'patch'}, use_global_device_ids=true, to_apply=%region_2.3 | all-reduce | flops 8 | bytes 64 | tf_op jit(solution)/shard_map/psum | solution.py:53
  20.1 6.6 %psum.43 = f32[8]{0:T(128)S(1)} all-reduce(f32[8]{0:T(128)S(1)} %reduce_sum.112), channel_id=1, replica_groups=mesh['groups'=2,'patch'=4,'chan'=2,'sub'=2] {'patch'}, use_global_device_ids=true, to_apply=%region_5.6 | all-reduce | flops 8 | bytes 64 | tf_op jit(solution)/shard_map/psum | solution.py:55
  28.0 10.4 %all_gather.36 = bf16[640,256]{1,0:T(8,128)(2,1)S(1)} all-gather(bf16[160,256]{1,0:T(8,128)(2,1)S(1)} %fusion.115), channel_id=1, replica_groups=mesh['groups'=2,'patch'=4,'chan'=2,'sub'=2] {'chan','sub'}, dimensions={0}, use_global_device_ids=true | all-gather | bytes 409600 | tf_op jit(solution)/shard_map/all_gather | solution.py:63
  39.7 4.2 %collective-permute-start.1 = (bf16[640,1,256]{2,0,1:T(8,128)(2,1)S(1)}, bf16[640,1,256]{2,0,1:T(8,128)(2,1)S(1)}, u32[]{:S(2)}, u32[]{:S(2)}) collective-permute-start(bf16[640,1,256]{2,0,1:T(8,128)(2,1)S(1)} %bitcast.251), channel_id=1, source_target_pairs={{0,4},{4,8},{8,12},{1,5},{5,9},{9,13},{2,6},{6,10},{10,14},{3,7},{... | collective-permute-start | bytes 983048 | tf_op jit(solution)/shard_map/ppermute | solution.py:24
  46.5 3.5 %collective-permute-done.2 = bf16[640,1,256]{2,0,1:T(8,128)(2,1)S(1)} collective-permute-done((bf16[640,1,256]{2,0,1:T(8,128)(2,1)S(1)}, bf16[640,1,256]{2,0,1:T(8,128)(2,1)S(1)}, u32[]{:S(2)}, u32[]{:S(2)}) %collective-permute-start.2) | collective-permute-done | bytes 327712 | tf_op jit(solution)/shard_map/ppermute | solution.py:26
  53.0 1.3 fusion.59
  55.5 1.4 fusion.128
  57.1 9.8 %psum.44 = f32[8]{0:T(128)S(1)} all-reduce(f32[8]{0:T(128)S(1)} %reduce_sum.140), channel_id=1, replica_groups=mesh['groups'=2,'patch'=4,'chan'=2,'sub'=2] {'patch'}, use_global_device_ids=true, to_apply=%region_8.9 | all-reduce | flops 8 | bytes 64 | tf_op jit(solution)/shard_map/psum | solution.py:53
  67.4 6.6 %psum.45 = f32[8]{0:T(128)S(1)} all-reduce(f32[8]{0:T(128)S(1)} %reduce_sum.143), channel_id=1, replica_groups=mesh['groups'=2,'patch'=4,'chan'=2,'sub'=2] {'patch'}, use_global_device_ids=true, to_apply=%region_11.12 | all-reduce | flops 8 | bytes 64 | tf_op jit(solution)/shard_map/psum | solution.py:55
  74.4 10.5 %all_gather.37 = bf16[640,256]{1,0:T(8,128)(2,1)S(1)} all-gather(bf16[160,256]{1,0:T(8,128)(2,1)S(1)} %fusion.120), channel_id=1, replica_groups=mesh['groups'=2,'patch'=4,'chan'=2,'sub'=2] {'chan','sub'}, dimensions={0}, use_global_device_ids=true | all-gather | bytes 409600 | tf_op jit(solution)/shard_map/all_gather | solution.py:63
  86.2 4.2 %collective-permute-start.3 = (bf16[640,1,256]{2,0,1:T(8,128)(2,1)S(1)}, bf16[640,1,256]{2,0,1:T(8,128)(2,1)S(1)}, u32[]{:S(2)}, u32[]{:S(2)}) collective-permute-start(bf16[640,1,256]{2,0,1:T(8,128)(2,1)S(1)} %bitcast.254), channel_id=1, source_target_pairs={{0,4},{4,8},{8,12},{1,5},{5,9},{9,13},{2,6},{6,10},{10,14},{3,7},{... | collective-permute-start | bytes 983048 | tf_op jit(solution)/shard_map/ppermute | solution.py:24
  90.7 5.8 %collective-permute-done.4 = bf16[640,1,256]{2,0,1:T(8,128)(2,1)S(1)} collective-permute-done((bf16[640,1,256]{2,0,1:T(8,128)(2,1)S(1)}, bf16[640,1,256]{2,0,1:T(8,128)(2,1)S(1)}, u32[]{:S(2)}, u32[]{:S(2)}) %collective-permute-start.4) | collective-permute-done | bytes 327712 | tf_op jit(solution)/shard_map/ppermute | solution.py:26
  100.1 1.4 fusion.129
  101.7 9.8 %psum.46 = f32[8]{0:T(128)S(1)} all-reduce(f32[8]{0:T(128)S(1)} %reduce_sum.146), channel_id=1, replica_groups=mesh['groups'=2,'patch'=4,'chan'=2,'sub'=2] {'patch'}, use_global_device_ids=true, to_apply=%region_14.15 | all-reduce | flops 8 | bytes 64 | tf_op jit(solution)/shard_map/psum | solution.py:53
  112.1 6.6 %psum.47 = f32[8]{0:T(128)S(1)} all-reduce(f32[8]{0:T(128)S(1)} %reduce_sum.149), channel_id=1, replica_groups=mesh['groups'=2,'patch'=4,'chan'=2,'sub'=2] {'patch'}, use_global_device_ids=true, to_apply=%region_17.18 | all-reduce | flops 8 | bytes 64 | tf_op jit(solution)/shard_map/psum | solution.py:55
  119.0 10.5 %all_gather.38 = bf16[640,256]{1,0:T(8,128)(2,1)S(1)} all-gather(bf16[160,256]{1,0:T(8,128)(2,1)S(1)} %multiply_convert_fusion), channel_id=1, replica_groups=mesh['groups'=2,'patch'=4,'chan'=2,'sub'=2] {'chan','sub'}, dimensions={0}, use_global_device_ids=true | all-gather | bytes 409600 | tf_op jit(solution)/shard_map/all_gather | solution.py:114
  129.7 6.2 %all_gather.39 = bf16[640,256]{1,0:T(8,128)(2,1)S(1)} all-gather(bf16[160,256]{1,0:T(8,128)(2,1)S(1)} %fusion.34), channel_id=1, replica_groups=mesh['groups'=2,'patch'=4,'chan'=2,'sub'=2] {'chan','sub'}, dimensions={0}, use_global_device_ids=true | all-gather | bytes 409600 | tf_op jit(solution)/shard_map/all_gather | solution.py:117
  138.2 3.5 %all-to-all-start = ((bf16[2,256,160]{2,0,1:T(2,128)(2,1)}), bf16[2,256,160]{2,0,1:T(2,128)(2,1)S(1)}, u32[]{:S(2)}, u32[]{:S(2)}) async-start(bf16[2,256,160]{2,0,1:T(2,128)(2,1)} %copy.35), calls=%async_computation | async-start | bytes 524288 | tf_op jit(solution)/shard_map/all_to_all | solution.py:130
  141.7 8.5 %all_gather.40 = bf16[640,256]{1,0:T(8,128)(2,1)S(1)} all-gather(bf16[160,256]{1,0:T(8,128)(2,1)S(1)} %fusion.33), channel_id=1, replica_groups=mesh['groups'=2,'patch'=4,'chan'=2,'sub'=2] {'chan','sub'}, dimensions={0}, use_global_device_ids=true | all-gather | bytes 409600 | tf_op jit(solution)/shard_map/all_gather | solution.py:124
  151.5 33.1 %while.35 = (s32[]{:T(128)}, f32[10,256]{1,0:T(8,128)S(1)}, f32[10,256]{1,0:T(8,128)S(1)}, f32[10,64,256]{2,1,0:T(8,128)S(1)}, bf16[2,64,640]{1,2,0:T(8,128)(2,1...) while((s32[]{:T(128)}, f32[10,256]{1,0:T(8,128)S(1)}, f32[10,256]{1,0:T(8,128)S(1)}, ...), condition=%wide.region_25.26_spmd, body=%wide.region_22.25_spmd.sunk | while | flops 43095040 | bytes 5242997 | solution.py:163
  151.5 1.7 collective-permute-start
  153.3 9.3 %collective-permute-done = bf16[2,64,640]{1,2,0:T(8,128)(2,1)S(1)} collective-permute-done((bf16[2,64,640]{1,2,0:T(8,128)(2,1)S(1)}, bf16[2,64,640]{1,2,0:T(8,128)(2,1)S(1)}, u32[]{:S(2)}, u32[]{:S(2)}) %collective-permute-start) | collective-permute-done | bytes 163872 | tf_op jit(solution)/shard_map/while/body/eval_jaxpr/ppermute | solution.py:35
  163.6 10.0 %collective-permute-done = bf16[2,64,640]{1,2,0:T(8,128)(2,1)S(1)} collective-permute-done((bf16[2,64,640]{1,2,0:T(8,128)(2,1)S(1)}, bf16[2,64,640]{1,2,0:T(8,128)(2,1)S(1)}, u32[]{:S(2)}, u32[]{:S(2)}) %collective-permute-start) | collective-permute-done | bytes 163872 | tf_op jit(solution)/shard_map/while/body/eval_jaxpr/ppermute | solution.py:35
  174.6 9.1 %collective-permute-done = bf16[2,64,640]{1,2,0:T(8,128)(2,1)S(1)} collective-permute-done((bf16[2,64,640]{1,2,0:T(8,128)(2,1)S(1)}, bf16[2,64,640]{1,2,0:T(8,128)(2,1)S(1)}, u32[]{:S(2)}, u32[]{:S(2)}) %collective-permute-start) | collective-permute-done | bytes 163872 | tf_op jit(solution)/shard_map/while/body/eval_jaxpr/ppermute | solution.py:35
  185.5 7.9 %all-gather.3 = f32[4,10,256]{2,1,0:T(8,128)S(1)} all-gather(f32[1,10,256]{2,1,0:T(8,128)S(1)} %bitcast.249), channel_id=2, replica_groups=mesh['groups'=2,'patch'=4,'chan'=2,'sub'=2] {'chan','sub'}, dimensions={0}, use_global_device_ids=true | all-gather | bytes 51200 | tf_op jit(solution)/shard_map/all_gather | solution.py:39
  193.4 5.6 %all-gather.4 = f32[4,10,256]{2,1,0:T(8,128)S(1)} all-gather(f32[1,10,256]{2,1,0:T(8,128)S(1)} %bitcast.259), channel_id=3, replica_groups=mesh['groups'=2,'patch'=4,'chan'=2,'sub'=2] {'chan','sub'}, dimensions={0}, use_global_device_ids=true | all-gather | bytes 51200 | tf_op jit(solution)/shard_map/all_gather | solution.py:39
  199.0 12.5 %all-gather.7.cloned.1.call-done = f32[40,64,256]{2,1,0:T(8,128)} async-done(((f32[10,64,256]{2,1,0:T(8,128)}), f32[40,64,256]{2,1,0:T(8,128)}) %all-gather.7.cloned.1.call-update) | async-done | bytes 2621456 | tf_op jit(solution)/shard_map/all_gather | solution.py:39
  212.6 4.3 %while.36 = (s32[]{:T(128)}, f32[10,256]{1,0:T(8,128)S(1)}, f32[10,256]{1,0:T(8,128)S(1)}, f32[10,64,256]{2,1,0:T(8,128)S(1)}, f32[4,10,256]{2,1,0:T(8,128)S(1)}...) while((s32[]{:T(128)}, f32[10,256]{1,0:T(8,128)S(1)}, ...), condition=%wide.region_27.28_spmd, body=%wide.region_26.27_spmd.sunk | while | flops 506885 | bytes 2068623 | solution.py:45
  212.6 1.4 fusion.171
  214.1 1.4 fusion.171
  215.5 1.4 fusion.171
  217.2 6.2 %all_gather.47 = bf16[640,256]{1,0:T(8,128)(2,1)S(1)} all-gather(bf16[160,256]{1,0:T(8,128)(2,1)S(1)} %fusion.31), channel_id=1, replica_groups=mesh['groups'=2,'patch'=4,'chan'=2,'sub'=2] {'chan','sub'}, dimensions={0}, use_global_device_ids=true | all-gather | bytes 409600 | tf_op jit(solution)/shard_map/all_gather | solution.py:174
  (141 shorter events, 28.3 us)
Async XLA Ops:
  6.5 38.2 %copy-start = (bf16[1280,320]{0,1:T(8,128)(2,1)S(1)}, bf16[1280,320]{0,1:T(8,128)(2,1)}, u32[]{:S(2)}) copy-start(bf16[1280,320]{0,1:T(8,128)(2,1)} %param.17) | copy-start | bytes 2457604
  6.5 39.6 %copy-start.4 = (bf16[9,160,640]{2,1,0:T(8,128)(2,1)S(1)}, bf16[9,160,640]{2,1,0:T(8,128)(2,1)}, u32[]{:S(2)}) copy-start(bf16[9,160,640]{2,1,0:T(8,128)(2,1)} %param.19) | copy-start | bytes 5529604
  38.4 11.5 %collective-permute-start.2 = (bf16[640,1,256]{2,0,1:T(8,128)(2,1)S(1)}, bf16[640,1,256]{2,0,1:T(8,128)(2,1)S(1)}, u32[]{:S(2)}, u32[]{:S(2)}) collective-permute-start(bf16[640,1,256]{2,0,1:T(8,128)(2,1)S(1)} %bitcast.250), channel_id=1, source_target_pairs={{4,0},{8,4},{12,8},{5,1},{9,5},{13,9},{6,2},{10,6},{14,10},{7,3},{... | collective-permute-start | bytes 983048 | tf_op jit(solution)/shard_map/ppermute | solution.py:26
  39.7 11.1 %collective-permute-start.1 = (bf16[640,1,256]{2,0,1:T(8,128)(2,1)S(1)}, bf16[640,1,256]{2,0,1:T(8,128)(2,1)S(1)}, u32[]{:S(2)}, u32[]{:S(2)}) collective-permute-start(bf16[640,1,256]{2,0,1:T(8,128)(2,1)S(1)} %bitcast.251), channel_id=1, source_target_pairs={{0,4},{4,8},{8,12},{1,5},{5,9},{9,13},{2,6},{6,10},{10,14},{3,7},{... | collective-permute-start | bytes 983048 | tf_op jit(solution)/shard_map/ppermute | solution.py:24
  53.0 37.4 %copy-start.3 = (bf16[9,160,640]{2,1,0:T(8,128)(2,1)S(1)}, bf16[9,160,640]{2,1,0:T(8,128)(2,1)}, u32[]{:S(2)}) copy-start(bf16[9,160,640]{2,1,0:T(8,128)(2,1)} %param.20) | copy-start | bytes 5529604
  84.9 11.5 %collective-permute-start.4 = (bf16[640,1,256]{2,0,1:T(8,128)(2,1)S(1)}, bf16[640,1,256]{2,0,1:T(8,128)(2,1)S(1)}, u32[]{:S(2)}, u32[]{:S(2)}) collective-permute-start(bf16[640,1,256]{2,0,1:T(8,128)(2,1)S(1)} %bitcast.253), channel_id=1, source_target_pairs={{4,0},{8,4},{12,8},{5,1},{9,5},{13,9},{6,2},{10,6},{14,10},{7,3},{... | collective-permute-start | bytes 983048 | tf_op jit(solution)/shard_map/ppermute | solution.py:26
  86.2 11.1 %collective-permute-start.3 = (bf16[640,1,256]{2,0,1:T(8,128)(2,1)S(1)}, bf16[640,1,256]{2,0,1:T(8,128)(2,1)S(1)}, u32[]{:S(2)}, u32[]{:S(2)}) collective-permute-start(bf16[640,1,256]{2,0,1:T(8,128)(2,1)S(1)} %bitcast.254), channel_id=1, source_target_pairs={{0,4},{4,8},{8,12},{1,5},{5,9},{9,13},{2,6},{6,10},{10,14},{3,7},{... | collective-permute-start | bytes 983048 | tf_op jit(solution)/shard_map/ppermute | solution.py:24
  99.0 1.1 copy-start.2
  99.6 29.9 %copy-start.5 = (bf16[160,640]{1,0:T(8,128)(2,1)S(1)}, bf16[160,640]{1,0:T(8,128)(2,1)}, u32[]{:S(2)}) copy-start(bf16[160,640]{1,0:T(8,128)(2,1)} %param.21) | copy-start | bytes 614404
  100.1 36.1 %copy-start.9 = (bf16[160,640]{1,0:T(8,128)(2,1)S(1)}, bf16[160,640]{1,0:T(8,128)(2,1)}, u32[]{:S(2)}) copy-start(bf16[160,640]{1,0:T(8,128)(2,1)} %param.22) | copy-start | bytes 614404
  136.0 1.0 copy-start.8
  138.2 12.0 %all-to-all-start = ((bf16[2,256,160]{2,0,1:T(2,128)(2,1)}), bf16[2,256,160]{2,0,1:T(2,128)(2,1)S(1)}, u32[]{:S(2)}, u32[]{:S(2)}) async-start(bf16[2,256,160]{2,0,1:T(2,128)(2,1)} %copy.35), calls=%async_computation | async-start | bytes 524288 | tf_op jit(solution)/shard_map/all_to_all | solution.py:130
  141.7 69.7 %all-gather.7.cloned.1.call-start = ((), (), s32[]{:S(2)}) async-start(), calls=%async_computation.1 | async-start | bytes 3276800 | tf_op jit(solution)/shard_map/all_gather | solution.py:39
  151.5 11.0 %collective-permute-start = (bf16[2,64,640]{1,2,0:T(8,128)(2,1)S(1)}, bf16[2,64,640]{1,2,0:T(8,128)(2,1)S(1)}, u32[]{:S(2)}, u32[]{:S(2)}) collective-permute-start(bf16[2,64,640]{1,2,0:T(8,128)(2,1)S(1)} %get-tuple-element.398), channel_id=1, source_target_pairs={{0,4},{4,8},{8,12},{12,0},{1,5},{5,9},{9,13},{13,1},{2,6},{6,10},{... | collective-permute-start | bytes 491528 | tf_op jit(solution)/shard_map/while/body/eval_jaxpr/ppermute | solution.py:35
  163.5 10.1 %collective-permute-start = (bf16[2,64,640]{1,2,0:T(8,128)(2,1)S(1)}, bf16[2,64,640]{1,2,0:T(8,128)(2,1)S(1)}, u32[]{:S(2)}, u32[]{:S(2)}) collective-permute-start(bf16[2,64,640]{1,2,0:T(8,128)(2,1)S(1)} %get-tuple-element.398), channel_id=1, source_target_pairs={{0,4},{4,8},{8,12},{12,0},{1,5},{5,9},{9,13},{13,1},{2,6},{6,10},{... | collective-permute-start | bytes 491528 | tf_op jit(solution)/shard_map/while/body/eval_jaxpr/ppermute | solution.py:35
  174.5 9.2 %collective-permute-start = (bf16[2,64,640]{1,2,0:T(8,128)(2,1)S(1)}, bf16[2,64,640]{1,2,0:T(8,128)(2,1)S(1)}, u32[]{:S(2)}, u32[]{:S(2)}) collective-permute-start(bf16[2,64,640]{1,2,0:T(8,128)(2,1)S(1)} %get-tuple-element.398), channel_id=1, source_target_pairs={{0,4},{4,8},{8,12},{12,0},{1,5},{5,9},{9,13},{13,1},{2,6},{6,10},{... | collective-permute-start | bytes 491528 | tf_op jit(solution)/shard_map/while/body/eval_jaxpr/ppermute | solution.py:35
  184.7 0.8 copy-start.1
  212.6 4.4 %copy-start.6 = (bf16[160,640]{1,0:T(8,128)(2,1)S(1)}, bf16[160,640]{1,0:T(8,128)(2,1)}, u32[]{:S(2)}) copy-start(bf16[160,640]{1,0:T(8,128)(2,1)} %param.24) | copy-start | bytes 614404
  216.9 6.5 %copy-start.7 = (bf16[160,640]{1,0:T(8,128)(2,1)S(1)}, bf16[160,640]{1,0:T(8,128)(2,1)}, u32[]{:S(2)}) copy-start(bf16[160,640]{1,0:T(8,128)(2,1)} %param.25) | copy-start | bytes 614404
Sparse Core Ops, SparseCore 0:
  185.7 25.7 all-gather.6
where the time goes:
time: 232 us; the launch traced here: 231 us
  blocking collectives  116 us (50%)
  waiting for transfers between devices  51.8 us (22%)
  starting transfers between devices  16.4 us (7%)
  matrix products  15 us (6%)
  between operations  14.5 us (6%)
  other arithmetic  11.6 us (5%)
  local copies, waits for them, and re-layouts  5.52 us (2%)
    psum x3, blocking collectives, group_norm(): centre = lax.psum(jnp.sum(grouped, axis=(1, 2)), 'patch') / cell_count  30.3 us
    ppermute x3, waiting for transfers between devices, from_behind(): lax.ppermute(array, axis, [(i, (i + by) % count) for i in range(count)])  28.4 us
    all_gather x2, blocking collectives, convolve(): whole_rows = lax.all_gather(active, ('chan', 'sub'), axis=0, tiled=True)  20.9 us
    psum x3, blocking collectives, group_norm(): lax.psum(jnp.sum(shifted * shifted, axis=(1, 2)), 'patch') / cell_count  19.9 us
    all_gather x2, blocking collectives, merged(): everything = jax.tree.map(lambda part: lax.all_gather(part, axis), array)  13.4 us
    all_gather x1, waiting for transfers between devices, merged(): everything = jax.tree.map(lambda part: lax.all_gather(part, axis), array)  12.5 us
    all_gather x1, blocking collectives, local(): lax.all_gather(normed, ('chan', 'sub'), axis=0, tiled=True)  10.5 us
    ppermute x2, waiting for transfers between devices, with_halo(): lax.ppermute(head, axis, [((i + 1) % count, i) for i in range(ends)])  9.22 us
  transfers between devices with their start and end apart: 9, of which 8 were waited for; matrix products, arithmetic and copies ran while one was open for 1% of the time, Pallas kernels for 0%

commit v1 on v0

v1 whole, which is shorter than its diff:
```python
import functools
import math

import jax
import jax.numpy as jnp
from jax import lax
from jax.experimental import pallas as pl
from jax.experimental.pallas import tpu as pltpu
from jax.sharding import PartitionSpec as P

C = 640
HEADS = 10
HEAD_DIM = 64
NGROUPS = 32
FREQ = 320
WIDTH = 256
GROUP = C // NGROUPS
MESH = pl.DeviceIdType.MESH
F32 = jnp.float32
BF16 = jnp.bfloat16
HIGH = lax.Precision.HIGHEST

G_PW, G_OW, G_Q, G_K, G_V, G_X1, G_X2, G_X3, G_AT, G_S1, G_S2, G_S3 = range(12)
G_LN = 12


def dot(a, b, precision=None):
    return jnp.dot(a, b, preferred_element_type=F32, precision=precision)


def dot_nt(a, b):
    return lax.dot_general(a, b, (((1,), (1,)), ((), ())), preferred_element_type=F32)


def dot_tn(a, b):
    return lax.dot_general(a, b, (((0,), (0,)), ((), ())), preferred_element_type=F32)


def loop(low, high, body):
    if high - low <= 4:
        for k in range(low, high):
            body(k)
    else:
        lax.fori_loop(low, high, lambda k, _: (body(k), 0)[1], 0)


def silu(v):
    return v / (1.0 + jnp.exp(-v))


def kernel(
    npatch, nchan, nsub, own, nheads,
    latent, emb, time_w1, time_proj, conv1_w, conv2_w, proj_in_w, q_w, kv_w, out_w, proj_out_w,
    out,
    tw1, tpj, cw1, cw2, po, pw, ow, qw, kw, vw, x1, x2, x3, at, zst, cst, hsend, hrecv,
    ln, vals, scores, attn, proj, res,
    lsem, gsend, grecv, zsend, zrecv, hssem, hrsem, lnsend, lnrecv,
):
    band = lax.axis_index("patch")
    chan = lax.axis_index("chan")
    sub = lax.axis_index("sub")
    idx = chan * nsub + sub
    nidx = nchan * nsub
    tokens = latent.shape[1]
    aligned = (own * nsub) % HEAD_DIM == 0

    def rows(block, size):
        return pl.ds(pl.multiple_of(block * size, size if size == 8 else 16), size)

    mine = rows(idx, own)
    pairs = [
        (conv1_w, cw1), (time_w1, tw1), (time_proj, tpj), (q_w, qw.at[mine]),
        (kv_w.at[0], kw.at[mine]), (kv_w.at[1], vw.at[mine]), (proj_in_w, pw.at[mine]),
        (conv2_w, cw2), (out_w, ow.at[mine]), (proj_out_w, po),
    ]
    loads = [pltpu.make_async_copy(a, b, lsem.at[i]) for i, (a, b) in enumerate(pairs)]
    L_C1, L_T1, L_TP, L_Q, L_K, L_V, L_PW, L_C2, L_OW, L_PO = loads
    for load in loads:
        load.start()

    def other(k, by, count):
        return lax.rem(k + by + count, count)

    class Gather:
        def __init__(self, g, buf, size, only_sub=False):
            self.g, self.buf, self.size = g, buf, size
            self.chans = 1 if only_sub else nchan

        def copy(self, block, d, s):
            ref = self.buf.at[rows(block, self.size)]
            to = {"chan": other(chan, d, nchan)} if s == 0 else {"sub": other(sub, s, nsub)}
            return pltpu.make_async_remote_copy(
                src_ref=ref, dst_ref=ref, send_sem=gsend.at[self.g, d, s],
                recv_sem=grecv.at[self.g, d, s], device_id=to, device_id_type=MESH,
            )

        def start(self):
            for d in range(1, self.chans):
                self.copy(idx, d, 0).start()
            for s in range(1, nsub):
                self.copy(idx, 0, s).start()

        def forward(self):
            for d in range(1, self.chans):
                block = other(chan, -d, nchan) * nsub + sub
                self.copy(block, d, 0).wait_recv()
                for s in range(1, nsub):
                    self.copy(block, d, s).start()

        def finish(self):
            for d in range(self.chans):
                for s in range(1, nsub):
                    block = other(chan, -d, nchan) * nsub + other(sub, -s, nsub)
                    self.copy(block, d, s).wait_recv()

        def drain(self):
            for d in range(self.chans):
                for s in range(nsub):
                    if d or s:
                        self.copy(idx, d, s).wait_send()

    gw = [
        Gather(G_Q, qw, own, aligned), Gather(G_K, kw, own, aligned), Gather(G_V, vw, own, aligned),
    ]
    gpw, gow = Gather(G_PW, pw, own), Gather(G_OW, ow, own)
    gx = [Gather(G_X1, x1, own), Gather(G_X2, x2, own), Gather(G_X3, x3, own)]
    gat = Gather(G_AT, at, own)
    gst = [Gather(G_S1 + i, cst.at[i], 8) for i in range(3)]

    cell = GROUP * tokens

    def members(shape, group_dim, size):
        gi = lax.broadcasted_iota(jnp.int32, shape, group_dim)
        ci = lax.broadcasted_iota(jnp.int32, shape, 1 - group_dim)
        g = gi & 7
        first = (gi >> 3) * size + g * GROUP
        inside = (ci >= first) & (ci < first + GROUP) & (g < size // GROUP)
        return jnp.where(inside, 1.0, 0.0).astype(F32)

    def stats(x, layer):
        e = members((8, own), 0, own)
        et = members((own, 8), 1, own)
        mean = jnp.sum(dot(e, x, HIGH), axis=1, keepdims=True) * (1.0 / cell)
        mean = jnp.broadcast_to(mean, (8, 128))
        mc = dot(et, mean, HIGH)
        dev = x - jnp.concatenate([mc] * (tokens // 128), axis=1)
        m2 = jnp.sum(dot(e, dev * dev, HIGH), axis=1, keepdims=True)
        lane = lax.broadcasted_iota(jnp.int32, (8, 128), 1)
        zst[layer, band] = jnp.where(lane < 64, mean, m2)

    def zcopy(layer, o):
        ref = zst.at[layer, band]
        return pltpu.make_async_remote_copy(
            src_ref=ref, dst_ref=ref, send_sem=zsend.at[layer, o], recv_sem=zrecv.at[layer, o],
            device_id={"patch": other(band, o, npatch)}, device_id_type=MESH,
        )

    def zarrived(layer, o):
        ref = zst.at[layer, other(band, -o, npatch)]
        pltpu.make_async_remote_copy(
            src_ref=ref, dst_ref=ref, send_sem=zsend.at[layer, o], recv_sem=zrecv.at[layer, o],
            device_id={"patch": other(band, o, npatch)}, device_id_type=MESH,
        ).wait_recv()

    def combined(layer, eps):
        loop(1, npatch, lambda o: zarrived(layer, o))
        tile = zst[layer]
        means, m2s = tile[:, :, 0:1], tile[:, :, 127:128]
        mean = jnp.sum(means, axis=0) * (1.0 / npatch)
        dev = means - mean[None]
        var = jnp.sum(m2s + cell * (dev * dev), axis=0) * (1.0 / (cell * npatch))
        lane = lax.broadcasted_iota(jnp.int32, (8, 128), 1)
        cst[layer, rows(idx, 8)] = jnp.where(
            lane < 64, jnp.broadcast_to(mean, (8, 128)),
            jnp.broadcast_to(lax.rsqrt(var + eps), (8, 128)),
        )
        gst[layer].start()

    def normalize(x, layer):
        both = dot(members((C, nidx * 8), 1, own), cst[layer], HIGH)
        return (x.astype(F32) - both[:, 0:1]) * both[:, 64:65]

    def hcopy(layer, way):
        return pltpu.make_async_remote_copy(
            src_ref=hsend.at[layer, way], dst_ref=hrecv.at[layer, way],
            send_sem=hssem.at[layer, way], recv_sem=hrsem.at[layer, way],
            device_id={"patch": other(band, 1 - 2 * way, npatch)}, device_id_type=MESH,
        )

    has_above, has_below = band > 0, band < npatch - 1

    def convolve(act, weight, layer):
        col = lax.broadcasted_iota(jnp.int32, act.shape, 1)
        taps = [
            jnp.where(col == 0, 0.0, pltpu.roll(act, 1, 1)).astype(BF16),
            act.astype(BF16),
            jnp.where(col == tokens - 1, 0.0, pltpu.roll(act, tokens - 1, 1)).astype(BF16),
        ]

        def row(i):
            return sum(dot(weight[3 * i + j], taps[j]) for j in range(3))

        hsend[layer, 0] = row(0).astype(BF16)

        @pl.when(has_below)
        def _():
            hcopy(layer, 0).start()

        hsend[layer, 1] = row(2).astype(BF16)

        @pl.when(has_above)
        def _():
            hcopy(layer, 1).start()

        return row(1)

    def neighbours(layer):
        @pl.when(has_above)
        def _():
            hcopy(layer, 0).wait_recv()

        @pl.when(has_below)
        def _():
            hcopy(layer, 1).wait_recv()

        return hrecv[layer, 0].astype(F32) + hrecv[layer, 1].astype(F32)

    for layer in range(2):
        @pl.when(jnp.logical_not(has_above))
        def _():
            hrecv[layer, 0] = jnp.zeros((own, tokens), BF16)

        @pl.when(jnp.logical_not(has_below))
        def _():
            hrecv[layer, 1] = jnp.zeros((own, tokens), BF16)

    x1[mine, :] = latent[...]
    lat = latent[...].astype(F32)
    stats(lat, 0)

    barrier = pltpu.get_barrier_semaphore()
    for d in range(1, nchan):
        pl.semaphore_signal(barrier, inc=1, device_id={"chan": other(chan, d, nchan)}, device_id_type=MESH)
    for s in range(1, nsub):
        pl.semaphore_signal(barrier, inc=1, device_id={"sub": other(sub, s, nsub)}, device_id_type=MESH)
    loop(1, npatch, lambda o: pl.semaphore_signal(
        barrier, inc=1, device_id={"patch": other(band, o, npatch)}, device_id_type=MESH))
    pl.semaphore_wait(barrier, nchan + nsub + npatch - 3)

    loop(1, npatch, lambda o: zcopy(0, o).start())
    gx[0].start()
    L_T1.wait()
    hidden = silu(dot_nt(emb[...], tw1[...]))
    L_TP.wait()
    bias = dot_nt(tpj[...], silu(hidden).astype(BF16))
    gx[0].forward()
    combined(0, 1e-05)
    gst[0].forward()
    for load, g in zip((L_Q, L_K, L_V), gw):
        load.wait()
        g.start()
    gx[0].finish()
    gst[0].finish()
    L_PW.wait()
    gpw.start()
    L_C1.wait()
    centre = convolve(silu(normalize(x1[...], 0)), cw1, 0)
    conv_one = (centre + neighbours(0) + jnp.concatenate([bias] * (tokens // 128), axis=1)).astype(BF16)
    x2[mine, :] = conv_one
    stats(conv_one.astype(F32), 1)

    loop(1, npatch, lambda o: zcopy(1, o).start())
    gx[1].start()
    gpw.forward()
    gx[1].forward()
    combined(1, 1e-05)
    gst[1].forward()
    gx[1].finish()
    gst[1].finish()
    L_OW.wait()
    gow.start()
    L_C2.wait()
    centre = convolve(silu(normalize(x2[...], 1)), cw2, 1)
    resnet = (lat + (centre + neighbours(1))).astype(BF16)
    res[...] = resnet
    x3[mine, :] = resnet
    stats(resnet.astype(F32), 2)

    loop(1, npatch, lambda o: zcopy(2, o).start())
    gx[2].start()
    gow.forward()
    gx[2].forward()
    combined(2, 1e-06)
    gst[2].forward()
    gpw.finish()
    gx[2].finish()
    gst[2].finish()
    projected = dot(pw[...], normalize(x3[...], 2).astype(BF16)).astype(BF16)
    proj[...] = projected
    wide = projected.astype(F32)
    wide = wide - jnp.mean(wide, axis=0, keepdims=True)
    spread = jnp.mean(wide * wide, axis=0, keepdims=True)
    ln[band] = (wide * lax.rsqrt(spread + 1e-05)).astype(BF16)

    def lncopy(o, source):
        ref = ln.at[source, mine]
        return pltpu.make_async_remote_copy(
            src_ref=ref, dst_ref=ref, send_sem=lnsend.at[o], recv_sem=lnrecv.at[o],
            device_id={"patch": other(band, o, npatch)}, device_id_type=MESH,
        )

    def gln(o):
        return Gather(G_LN + o, ln.at[other(band, -o, npatch)], own)

    loop(1, npatch, lambda o: lncopy(o, band).start())
    for g in gw:
        if not aligned:
            g.forward()
        g.finish()

    head0 = (idx * own) // HEAD_DIM
    span = nheads * HEAD_DIM
    held = pl.ds(pl.multiple_of(head0 * HEAD_DIM, HEAD_DIM), span)
    query = (dot(qw[held, :], ln[band]) * 0.125).astype(BF16)

    def score(source):
        tokens_of = ln[source]
        keys = dot(kw[held, :], tokens_of).astype(BF16)
        vals[source] = dot(vw[held, :], tokens_of).astype(BF16)
        for h in range(nheads):
            part = slice(h * HEAD_DIM, (h + 1) * HEAD_DIM)
            scores[source, h] = dot_tn(keys[part], query[part])

    def relay(o):
        lncopy(o, other(band, -o, npatch)).wait_recv()
        gln(o).start()

    score(band)
    loop(1, npatch, relay)
    loop(1, npatch, lambda o: gln(o).forward())

    def arrive(o):
        gln(o).finish()
        score(other(band, -o, npatch))

    loop(1, npatch, arrive)

    for h in range(nheads):
        part = slice(h * HEAD_DIM, (h + 1) * HEAD_DIM)

        def peak_of(b, peak):
            return jnp.maximum(peak, jnp.max(scores[b, h], axis=0, keepdims=True))

        def add(b, so_far):
            total, weighted = so_far
            weights = jnp.exp(scores[b, h] - peak)
            total = total + jnp.sum(weights, axis=0, keepdims=True)
            return total, weighted + dot(vals[b, part], weights.astype(BF16))

        peak = jnp.full((1, tokens), -jnp.inf, F32)
        so_far = (jnp.zeros((1, tokens), F32), jnp.zeros((HEAD_DIM, tokens), F32))
        if npatch <= 4:
            for b in range(npatch):
                peak = peak_of(b, peak)
            for b in range(npatch):
                so_far = add(b, so_far)
        else:
            peak = lax.fori_loop(0, npatch, peak_of, peak)
            so_far = lax.fori_loop(0, npatch, add, so_far)
        attn[part, :] = (so_far[1] / so_far[0]).astype(BF16)

    skip = pl.multiple_of(idx * own - head0 * HEAD_DIM, 16)
    at[mine, :] = attn[pl.ds(skip, own), :]
    gat.start()
    gat.forward()
    gow.finish()
    gat.finish()
    mixed = (proj[...].astype(F32) + dot(ow[...], at[...])).astype(BF16)
    L_PO.wait()
    out[...] = (res[...].astype(F32) + dot(po[...], mixed)).astype(BF16)

    for g in gw + gx + gst + [gpw, gow, gat]:
        g.drain()
    loop(1, npatch, lambda o: gln(o).drain())
    loop(1, npatch, lambda o: lncopy(o, band).wait_send())
    for layer in range(3):
        loop(1, npatch, lambda o: zcopy(layer, o).wait_send())
    for layer in range(2):
        @pl.when(has_below)
        def _():
            hcopy(layer, 0).wait_send()

        @pl.when(has_above)
        def _():
            hcopy(layer, 1).wait_send()


def local(
    npatch, nchan, nsub,
    latent, timestep, time_w1, time_proj, conv1_w, conv2_w, proj_in_w, q_w, kv_w, out_w, proj_out_w,
):
    own, tokens = latent.shape
    nheads = -(-own // HEAD_DIM)
    nidx = nchan * nsub
    temb = time_w1.shape[0]
    half_width = FREQ // 2
    frequency = jnp.exp(-math.log(10000.0) * jnp.arange(half_width, dtype=F32) / half_width)
    angles = timestep[0].astype(F32) * frequency
    embedded = jnp.concatenate([jnp.cos(angles), jnp.sin(angles)]).astype(BF16)
    emb = jnp.broadcast_to(embedded[None, :], (128, FREQ))
    vmem = pl.BlockSpec(memory_space=pltpu.VMEM)
    hbm = pl.BlockSpec(memory_space=pl.ANY)
    dma = pltpu.SemaphoreType.DMA
    span = nheads * HEAD_DIM
    ngather = G_LN + npatch
    return pl.pallas_call(
        functools.partial(kernel, npatch, nchan, nsub, own, nheads),
        out_shape=jax.ShapeDtypeStruct((own, tokens), BF16),
        in_specs=[vmem, vmem] + [hbm] * 9,
        out_specs=vmem,
        scratch_shapes=[
            pltpu.VMEM((temb, FREQ), BF16),
            pltpu.VMEM((own, temb), BF16),
            pltpu.VMEM((9, own, C), BF16),
            pltpu.VMEM((9, own, C), BF16),
            pltpu.VMEM((own, C), BF16),
        ]
        + [pltpu.VMEM((C, C), BF16)] * 5
        + [pltpu.VMEM((C, tokens), BF16)] * 4
        + [
            pltpu.VMEM((3, npatch, 8, 128), F32),
            pltpu.VMEM((3, nidx * 8, 128), F32),
            pltpu.VMEM((2, 2, own, tokens), BF16),
            pltpu.VMEM((2, 2, own, tokens), BF16),
            pltpu.VMEM((npatch, C, tokens), BF16),
            pltpu.VMEM((npatch, span, tokens), BF16),
            pltpu.VMEM((npatch, nheads, tokens, tokens), F32),
            pltpu.VMEM((span, tokens), BF16),
            pltpu.VMEM((C, tokens), BF16),
            pltpu.VMEM((own, tokens), BF16),
            dma((10,)),
            dma((ngather, nchan, nsub)),
            dma((ngather, nchan, nsub)),
            dma((3, npatch)),
            dma((3, npatch)),
            dma((2, 2)),
            dma((2, 2)),
            dma((npatch,)),
            dma((npatch,)),
        ],
        compiler_params=pltpu.CompilerParams(
            collective_id=0, has_side_effects=True, vmem_limit_bytes=60 * 1024 * 1024
        ),
    )(
        latent, emb, time_w1, time_proj, conv1_w, conv2_w, proj_in_w, q_w, kv_w, out_w, proj_out_w
    )


def solution(mesh):
    in_specs = (
        P(("chan", "sub"), ("groups", "patch")),
        P("groups"),
        P(),
        P(("chan", "sub"), None),
        P(None, ("chan", "sub"), None),
        P(None, ("chan", "sub"), None),
        P(("chan", "sub"), None),
        P(("chan", "sub"), None),
        P(None, ("chan", "sub"), None),
        P(("chan", "sub"), None),
        P(("chan", "sub"), None),
    )
    out_specs = P(("chan", "sub"), ("groups", "patch"))
    sizes = [mesh.shape[a] for a in ("patch", "chan", "sub")]
    return jax.shard_map(
        functools.partial(local, *sizes), mesh=mesh, in_specs=in_specs, out_specs=out_specs, check_vma=False
    )
```

time: 232 us -> 70.7 us (0.30)
  blocking collectives: 116 us -> 0 us
  Pallas kernels: 0 us -> 65.3 us
  waiting for transfers between devices: 51.8 us -> 0 us
  starting transfers between devices: 16.4 us -> 0 us
  matrix products: 15 us -> 0 us
  between operations: 14.5 us -> 0.67 us
  other arithmetic: 11.6 us -> 0.13 us
    all_gather x8 -> x0, blocking collectives: 65.8 us -> none  [the longest x2 20.9 us: convolve(): whole_rows = lax.all_gather(active, ('chan', 'sub'), axis=0, tiled=True)]
    pallas_call x0 -> x1, Pallas kernels: none -> 65.3 us  [local(): pl.pallas_call(functools.partial(kernel, npatch, nchan, nsub, own, nheads...]
    psum x6 -> x0, blocking collectives: 50.2 us -> none  [the longest x3 30.3 us: group_norm(): centre = lax.psum(jnp.sum(grouped, axis=(1, 2)), 'patch') / cell_count]
    ppermute x7 -> x0, waiting for transfers between devices: 39.3 us -> none  [the longest x3 28.4 us: from_behind(): lax.ppermute(array, axis, [(i, (i + by) % count) for i in range(count)])]
    dot_general x33 -> x0, matrix products: 15 us -> none  [the longest x18 8.99 us: convolve(): jnp.dot(weight[offset], window, preferred_element_type=jnp.float32)]
    ppermute x7 -> x0, starting transfers between devices: 12.9 us -> none  [the longest x2 8.48 us: with_halo(): lax.ppermute(tail, axis, [(i, (i + 1) % count) for i in range(ends)])]
    all_gather x1 -> x0, waiting for transfers between devices: 12.5 us -> none  [merged(): everything = jax.tree.map(lambda part: lax.all_gather(part, axis), array)]
    add x9 -> x0, other arithmetic: 4.26 us -> none  [the longest x3 4.15 us: combine_parts(): sums_one * factor_one[:, None, :] + sums_two * factor_two[:, None, :]]
  transfers between devices with their start and end apart: 9 -> 0, of which waited for: 8 -> 0; matrix products, arithmetic and copies ran while one was open for 1% -> 0% of each run, Pallas kernels for 0% -> 0%
where the time goes in v1:
time: 70.7 us; the launch traced here: 70.5 us
  Pallas kernels  65.3 us (92%)
  local copies, waits for them, and re-layouts  4.4 us (6%)
    pallas_call x1, Pallas kernels, local(): pl.pallas_call(functools.partial(kernel, npatch, nchan, nsub, own, nheads...  65.3 us
    unnamed x2, local copies, waits for them, and re-layouts  3.74 us

profile of v1, /device:TPU:1, one launch (start us, length us, event | category | flops | bytes accessed | tf_op | source)
XLA Modules:
  0.0 70.5 jit_solution(381854209536526224)
XLA Ops:
  0.7 0.1 sine_convert_fusion
  0.7 0.1 pad_maximum_fusion
  0.8 0.7 broadcast_in_dim.2.emb
  1.4 2.2 %copy.12.time_w1 = bf16[1280,320]{1,0:T(8,128)(2,1)} copy(bf16[1280,320]{0,1:T(8,128)(2,1)} %param.13) | data formatting | bytes 1638400 | tf_op args[2]
  3.7 65.3 %shard_map.109 = bf16[160,256]{1,0:T(8,128)(2,1)} custom-call(bf16[160,256]{1,0:T(8,128)(2,1)} %latent.1, bf16[128,320]{1,0:T(8,128)(2,1)} %broadcast_in_dim.2.emb, bf16[1280,320]{1,0:T(8,128)(2,1)} %copy.12.time_w1, bf16[160,1280]{1,0:T(8,128)(2,1)} %time_proj.1, bf16[9,160,640]{2,1,0:T(8,128)(2,1)} %conv1_w.1, bf16[9,160,640]{2,1,0:T(8,128)(2,1)} %conv2_w.1, ...), custom_call_target="tpu_custom_call" | custom-call | tf_op jit(solution)/shard_map/pallas_call | solution.py:416
  69.0 1.5 %copy.15 = bf16[160,256]{1,0:T(8,128)(2,1)} copy(bf16[160,256]{1,0:T(8,128)(2,1)} %shard_map.109) | data formatting | bytes 163840

commit v2 on v1

--- a/solution.py
+++ b/solution.py
@@ -20,8 +20,8 @@
 BF16 = jnp.bfloat16
 HIGH = lax.Precision.HIGHEST
 
-G_PW, G_OW, G_Q, G_K, G_V, G_X1, G_X2, G_X3, G_AT, G_S1, G_S2, G_S3 = range(12)
-G_LN = 12
+G_PW, G_OW, G_Q, G_K, G_V, G_X1, G_X2, G_X3, G_AT = range(9)
+G_LN = 9
 
 
 def dot(a, b, precision=None):
@@ -37,7 +37,7 @@
 
 
 def loop(low, high, body):
-    if high - low <= 4:
+    if high - low <= 16:
         for k in range(low, high):
             body(k)
     else:
@@ -45,14 +45,15 @@
 
 
 def silu(v):
-    return v / (1.0 + jnp.exp(-v))
+    half = 0.5 * v
+    return half + half * jnp.tanh(half)
 
 
 def kernel(
     npatch, nchan, nsub, own, nheads,
     latent, emb, time_w1, time_proj, conv1_w, conv2_w, proj_in_w, q_w, kv_w, out_w, proj_out_w,
     out,
-    tw1, tpj, cw1, cw2, po, pw, ow, qw, kw, vw, x1, x2, x3, at, zst, cst, hsend, hrecv,
+    tw1, tpj, cw1, cw2, po, pw, ow, qw, kw, vw, x1, x2, x3, at, zst, hsend, hrecv,
     ln, vals, scores, attn, proj, res,
     lsem, gsend, grecv, zsend, zrecv, hssem, hrsem, lnsend, lnrecv,
 ):
@@ -65,7 +66,7 @@
     aligned = (own * nsub) % HEAD_DIM == 0
 
     def rows(block, size):
-        return pl.ds(pl.multiple_of(block * size, size if size == 8 else 16), size)
+        return pl.ds(pl.multiple_of(block * size, 16 if size % 16 == 0 else 8), size)
 
     mine = rows(idx, own)
     pairs = [
@@ -125,7 +126,6 @@
     gpw, gow = Gather(G_PW, pw, own), Gather(G_OW, ow, own)
     gx = [Gather(G_X1, x1, own), Gather(G_X2, x2, own), Gather(G_X3, x3, own)]
     gat = Gather(G_AT, at, own)
-    gst = [Gather(G_S1 + i, cst.at[i], 8) for i in range(3)]
 
     cell = GROUP * tokens
 
@@ -146,38 +146,44 @@
         dev = x - jnp.concatenate([mc] * (tokens // 128), axis=1)
         m2 = jnp.sum(dot(e, dev * dev, HIGH), axis=1, keepdims=True)
         lane = lax.broadcasted_iota(jnp.int32, (8, 128), 1)
-        zst[layer, band] = jnp.where(lane < 64, mean, m2)
-
-    def zcopy(layer, o):
-        ref = zst.at[layer, band]
+        zst[layer, band, rows(idx, 8)] = jnp.where(lane < 64, mean, m2)
+
+    everyone = npatch * nidx
+
+    def peer(p, way):
+        k = p % nidx
+        return {
+            "patch": other(band, way * (p // nidx), npatch),
+            "chan": other(chan, way * (k // nsub), nchan),
+            "sub": other(sub, way * (k % nsub), nsub),
+        }
+
+    def zcopy(layer, p, source=None):
+        b, k = (band, idx) if source is None else (source["patch"], source["chan"] * nsub + source["sub"])
+        ref = zst.at[layer, b, rows(k, 8)]
         return pltpu.make_async_remote_copy(
-            src_ref=ref, dst_ref=ref, send_sem=zsend.at[layer, o], recv_sem=zrecv.at[layer, o],
-            device_id={"patch": other(band, o, npatch)}, device_id_type=MESH,
+            src_ref=ref, dst_ref=ref, send_sem=zsend.at[layer, p], recv_sem=zrecv.at[layer, p],
+            device_id=peer(p, 1), device_id_type=MESH,
         )
 
-    def zarrived(layer, o):
-        ref = zst.at[layer, other(band, -o, npatch)]
-        pltpu.make_async_remote_copy(
-            src_ref=ref, dst_ref=ref, send_sem=zsend.at[layer, o], recv_sem=zrecv.at[layer, o],
-            device_id={"patch": other(band, o, npatch)}, device_id_type=MESH,
-        ).wait_recv()
+    def share(layer):
+        loop(1, everyone, lambda p: zcopy(layer, p).start())
 
     def combined(layer, eps):
-        loop(1, npatch, lambda o: zarrived(layer, o))
+        loop(1, everyone, lambda p: zcopy(layer, p, peer(p, -1)).wait_recv())
         tile = zst[layer]
         means, m2s = tile[:, :, 0:1], tile[:, :, 127:128]
         mean = jnp.sum(means, axis=0) * (1.0 / npatch)
         dev = means - mean[None]
         var = jnp.sum(m2s + cell * (dev * dev), axis=0) * (1.0 / (cell * npatch))
-        lane = lax.broadcasted_iota(jnp.int32, (8, 128), 1)
-        cst[layer, rows(idx, 8)] = jnp.where(
-            lane < 64, jnp.broadcast_to(mean, (8, 128)),
-            jnp.broadcast_to(lax.rsqrt(var + eps), (8, 128)),
+        shape = (nidx * 8, 128)
+        lane = lax.broadcasted_iota(jnp.int32, shape, 1)
+        pair = jnp.where(
+            lane < 64, jnp.broadcast_to(mean, shape), jnp.broadcast_to(lax.rsqrt(var + eps), shape)
         )
-        gst[layer].start()
-
-    def normalize(x, layer):
-        both = dot(members((C, nidx * 8), 1, own), cst[layer], HIGH)
+        return dot(members((C, nidx * 8), 1, own), pair, HIGH)
+
+    def normalize(x, both):
         return (x.astype(F32) - both[:, 0:1]) * both[:, 64:65]
 
     def hcopy(layer, way):
@@ -234,68 +240,58 @@
         def _():
             hrecv[layer, 1] = jnp.zeros((own, tokens), BF16)
 
+    barrier = pltpu.get_barrier_semaphore()
+    loop(1, everyone, lambda p: pl.semaphore_signal(
+        barrier, inc=1, device_id=peer(p, 1), device_id_type=MESH))
     x1[mine, :] = latent[...]
     lat = latent[...].astype(F32)
     stats(lat, 0)
 
-    barrier = pltpu.get_barrier_semaphore()
-    for d in range(1, nchan):
-        pl.semaphore_signal(barrier, inc=1, device_id={"chan": other(chan, d, nchan)}, device_id_type=MESH)
-    for s in range(1, nsub):
-        pl.semaphore_signal(barrier, inc=1, device_id={"sub": other(sub, s, nsub)}, device_id_type=MESH)
-    loop(1, npatch, lambda o: pl.semaphore_signal(
-        barrier, inc=1, device_id={"patch": other(band, o, npatch)}, device_id_type=MESH))
-    pl.semaphore_wait(barrier, nchan + nsub + npatch - 3)
-
-    loop(1, npatch, lambda o: zcopy(0, o).start())
+    pl.semaphore_wait(barrier, everyone - 1)
+
+    share(0)
     gx[0].start()
     L_T1.wait()
-    hidden = silu(dot_nt(emb[...], tw1[...]))
+    hidden = silu(dot(emb[...], tw1[...]))
     L_TP.wait()
     bias = dot_nt(tpj[...], silu(hidden).astype(BF16))
     gx[0].forward()
-    combined(0, 1e-05)
-    gst[0].forward()
+    norm = combined(0, 1e-05)
     for load, g in zip((L_Q, L_K, L_V), gw):
         load.wait()
         g.start()
     gx[0].finish()
-    gst[0].finish()
     L_PW.wait()
     gpw.start()
     L_C1.wait()
-    centre = convolve(silu(normalize(x1[...], 0)), cw1, 0)
-    conv_one = (centre + neighbours(0) + jnp.concatenate([bias] * (tokens // 128), axis=1)).astype(BF16)
+    centre = convolve(silu(normalize(x1[...], norm)), cw1, 0)
+    conv_one = (centre + neighbours(0) + bias[:, 0:1]).astype(BF16)
     x2[mine, :] = conv_one
     stats(conv_one.astype(F32), 1)
 
-    loop(1, npatch, lambda o: zcopy(1, o).start())
+    share(1)
     gx[1].start()
     gpw.forward()
     gx[1].forward()
-    combined(1, 1e-05)
-    gst[1].forward()
+    norm = combined(1, 1e-05)
     gx[1].finish()
-    gst[1].finish()
     L_OW.wait()
     gow.start()
     L_C2.wait()
-    centre = convolve(silu(normalize(x2[...], 1)), cw2, 1)
+    centre = convolve(silu(normalize(x2[...], norm)), cw2, 1)
     resnet = (lat + (centre + neighbours(1))).astype(BF16)
     res[...] = resnet
     x3[mine, :] = resnet
     stats(resnet.astype(F32), 2)
 
-    loop(1, npatch, lambda o: zcopy(2, o).start())
+    share(2)
     gx[2].start()
     gow.forward()
     gx[2].forward()
-    combined(2, 1e-06)
-    gst[2].forward()
+    norm = combined(2, 1e-06)
     gpw.finish()
     gx[2].finish()
-    gst[2].finish()
-    projected = dot(pw[...], normalize(x3[...], 2).astype(BF16)).astype(BF16)
+    projected = dot(pw[...], normalize(x3[...], norm).astype(BF16)).astype(BF16)
     proj[...] = projected
     wide = projected.astype(F32)
     wide = wide - jnp.mean(wide, axis=0, keepdims=True)
@@ -377,14 +373,14 @@
     gat.finish()
     mixed = (proj[...].astype(F32) + dot(ow[...], at[...])).astype(BF16)
     L_PO.wait()
-    out[...] = (res[...].astype(F32) + dot(po[...], mixed)).astype(BF16)
-
-    for g in gw + gx + gst + [gpw, gow, gat]:
+    out[...] = res[...].astype(F32) + dot(po[...], mixed)
+
+    for g in gw + gx + [gpw, gow, gat]:
         g.drain()
     loop(1, npatch, lambda o: gln(o).drain())
     loop(1, npatch, lambda o: lncopy(o, band).wait_send())
     for layer in range(3):
-        loop(1, npatch, lambda o: zcopy(layer, o).wait_send())
+        loop(1, everyone, lambda p: zcopy(layer, p).wait_send())
     for layer in range(2):
         @pl.when(has_below)
         def _():
@@ -407,19 +403,19 @@
     frequency = jnp.exp(-math.log(10000.0) * jnp.arange(half_width, dtype=F32) / half_width)
     angles = timestep[0].astype(F32) * frequency
     embedded = jnp.concatenate([jnp.cos(angles), jnp.sin(angles)]).astype(BF16)
-    emb = jnp.broadcast_to(embedded[None, :], (128, FREQ))
+    emb = jnp.broadcast_to(embedded[None, :], (16, FREQ))
     vmem = pl.BlockSpec(memory_space=pltpu.VMEM)
     hbm = pl.BlockSpec(memory_space=pl.ANY)
     dma = pltpu.SemaphoreType.DMA
     span = nheads * HEAD_DIM
     ngather = G_LN + npatch
-    return pl.pallas_call(
+    total = pl.pallas_call(
         functools.partial(kernel, npatch, nchan, nsub, own, nheads),
-        out_shape=jax.ShapeDtypeStruct((own, tokens), BF16),
+        out_shape=jax.ShapeDtypeStruct((own, tokens), F32),
         in_specs=[vmem, vmem] + [hbm] * 9,
         out_specs=vmem,
         scratch_shapes=[
-            pltpu.VMEM((temb, FREQ), BF16),
+            pltpu.VMEM((FREQ, temb), BF16),
             pltpu.VMEM((own, temb), BF16),
             pltpu.VMEM((9, own, C), BF16),
             pltpu.VMEM((9, own, C), BF16),
@@ -428,8 +424,7 @@
         + [pltpu.VMEM((C, C), BF16)] * 5
         + [pltpu.VMEM((C, tokens), BF16)] * 4
         + [
-            pltpu.VMEM((3, npatch, 8, 128), F32),
-            pltpu.VMEM((3, nidx * 8, 128), F32),
+            pltpu.VMEM((3, npatch, nidx * 8, 128), F32),
             pltpu.VMEM((2, 2, own, tokens), BF16),
             pltpu.VMEM((2, 2, own, tokens), BF16),
             pltpu.VMEM((npatch, C, tokens), BF16),
@@ -441,8 +436,8 @@
             dma((10,)),
             dma((ngather, nchan, nsub)),
             dma((ngather, nchan, nsub)),
-            dma((3, npatch)),
-            dma((3, npatch)),
+            dma((3, npatch * nidx)),
+            dma((3, npatch * nidx)),
             dma((2, 2)),
             dma((2, 2)),
             dma((npatch,)),
@@ -452,8 +447,9 @@
             collective_id=0, has_side_effects=True, vmem_limit_bytes=60 * 1024 * 1024
         ),
     )(
-        latent, emb, time_w1, time_proj, conv1_w, conv2_w, proj_in_w, q_w, kv_w, out_w, proj_out_w
+        latent, emb, time_w1.T, time_proj, conv1_w, conv2_w, proj_in_w, q_w, kv_w, out_w, proj_out_w
     )
+    return total.astype(BF16)
 
 
 def solution(mesh):

time: 70.7 us -> 61.6 us (0.87)
  Pallas kernels: 65.3 us -> 58.5 us
  local copies, waits for them, and re-layouts: 4.4 us -> 0.61 us
  other arithmetic: 0.13 us -> 1.69 us
    pallas_call x1, Pallas kernels: 65.3 us -> 58.5 us  [local(): pl.pallas_call(functools.partial(kernel, npatch, nchan, nsub, own, nheads...]
    unnamed x2 -> x0, local copies, waits for them, and re-layouts: 3.74 us -> none
    convert_element_type x0 -> x1, other arithmetic: none -> 1.56 us  [local(): return total.astype(BF16)]
where the time goes in v2:
time: 61.6 us; the launch traced here: 61.4 us
  Pallas kernels  58.5 us (95%)
  other arithmetic  1.69 us (3%)
  between operations  0.67 us (1%)
    pallas_call x1, Pallas kernels, local(): pl.pallas_call(functools.partial(kernel, npatch, nchan, nsub, own, nheads...  58.5 us
    convert_element_type x1, other arithmetic, local(): return total.astype(BF16)  1.56 us

profile of v2, /device:TPU:1, one launch (start us, length us, event | category | flops | bytes accessed | tf_op | source)
XLA Modules:
  0.0 61.4 jit_solution(2844341944621194496)
XLA Ops:
  0.7 0.1 sine_convert_fusion
  0.7 0.1 pad_maximum_fusion
  0.8 0.6 broadcast_in_dim.2.emb
  1.4 58.5 %shard_map.109 = f32[160,256]{1,0:T(8,128)} custom-call(bf16[160,256]{1,0:T(8,128)(2,1)} %latent.1, bf16[16,320]{1,0:T(8,128)(2,1)} %broadcast_in_dim.2.emb, bf16[320,1280]{1,0:T(8,128)(2,1)} %bitcast.2, bf16[160,1280]{1,0:T(8,128)(2,1)} %time_proj.1, bf16[9,160,640]{2,1,0:T(8,128)(2,1)} %conv1_w.1, bf16[9,160,640]{2,1,0:T(8,128)(2,1)} %conv2_w.1, ...), custom_call_target="tpu_custom_call" | custom-call | tf_op jit(solution)/shard_map/pallas_call | solution.py:412
  59.9 1.6 %convert_element_type.16 = bf16[160,256]{1,0:T(8,128)(2,1)} convert(f32[160,256]{1,0:T(8,128)} %shard_map.109) | non-fusion elementwise | flops 40960 | bytes 245760 | tf_op jit(solution)/shard_map/convert_element_type | solution.py:452

commit v3 on v2

--- a/solution.py
+++ b/solution.py
@@ -20,8 +20,8 @@
 BF16 = jnp.bfloat16
 HIGH = lax.Precision.HIGHEST
 
-G_PW, G_OW, G_Q, G_K, G_V, G_X1, G_X2, G_X3, G_AT = range(9)
-G_LN = 9
+G_PW, G_OW, G_Q, G_K, G_V, G_X1, G_X2, G_AT = range(8)
+G_LN = 8
 
 
 def dot(a, b, precision=None):
@@ -53,8 +53,8 @@
     npatch, nchan, nsub, own, nheads,
     latent, emb, time_w1, time_proj, conv1_w, conv2_w, proj_in_w, q_w, kv_w, out_w, proj_out_w,
     out,
-    tw1, tpj, cw1, cw2, po, pw, ow, qw, kw, vw, x1, x2, x3, at, zst, hsend, hrecv,
-    ln, vals, scores, attn, proj, res,
+    tw1, tpj, cw1, cw2, po, pw, ow, qw, kw, vw, x1, x2, at, zst, hsend, hrecv,
+    xr, qry, peaks, totals, sums, attn, proj, res,
     lsem, gsend, grecv, zsend, zrecv, hssem, hrsem, lnsend, lnrecv,
 ):
     band = lax.axis_index("patch")
@@ -124,7 +124,7 @@
         Gather(G_Q, qw, own, aligned), Gather(G_K, kw, own, aligned), Gather(G_V, vw, own, aligned),
     ]
     gpw, gow = Gather(G_PW, pw, own), Gather(G_OW, ow, own)
-    gx = [Gather(G_X1, x1, own), Gather(G_X2, x2, own), Gather(G_X3, x3, own)]
+    gx = [Gather(G_X1, x1, own), Gather(G_X2, x2, own)]
     gat = Gather(G_AT, at, own)
 
     cell = GROUP * tokens
@@ -281,89 +281,112 @@
     centre = convolve(silu(normalize(x2[...], norm)), cw2, 1)
     resnet = (lat + (centre + neighbours(1))).astype(BF16)
     res[...] = resnet
-    x3[mine, :] = resnet
+    xr[band, mine, :] = resnet
+
+    def zrow(to, source):
+        ref = xr.at[source, mine]
+        return pltpu.make_async_remote_copy(
+            src_ref=ref, dst_ref=ref, send_sem=lnsend.at[to], recv_sem=lnrecv.at[source],
+            device_id={"patch": to}, device_id_type=MESH,
+        )
+
+    def grow(source):
+        return Gather(G_LN + source, xr.at[source], own)
+
+    def nearest(rank):
+        near = jnp.minimum(band, npatch - 1 - band)
+        odd = rank % 2
+        step = (rank + odd) // 2
+        beyond = jnp.where(2 * band < npatch - 1, rank, npatch - 1 - rank)
+        return jnp.where(rank <= 2 * near, band + (1 - 2 * odd) * step, beyond)
+
+    grow(band).start()
+    loop(1, npatch, lambda r: zrow(nearest(r), band).start())
     stats(resnet.astype(F32), 2)
-
     share(2)
-    gx[2].start()
+    grow(band).forward()
     gow.forward()
-    gx[2].forward()
-    norm = combined(2, 1e-06)
     gpw.finish()
-    gx[2].finish()
-    projected = dot(pw[...], normalize(x3[...], norm).astype(BF16)).astype(BF16)
-    proj[...] = projected
-    wide = projected.astype(F32)
-    wide = wide - jnp.mean(wide, axis=0, keepdims=True)
-    spread = jnp.mean(wide * wide, axis=0, keepdims=True)
-    ln[band] = (wide * lax.rsqrt(spread + 1e-05)).astype(BF16)
-
-    def lncopy(o, source):
-        ref = ln.at[source, mine]
-        return pltpu.make_async_remote_copy(
-            src_ref=ref, dst_ref=ref, send_sem=lnsend.at[o], recv_sem=lnrecv.at[o],
-            device_id={"patch": other(band, o, npatch)}, device_id_type=MESH,
-        )
-
-    def gln(o):
-        return Gather(G_LN + o, ln.at[other(band, -o, npatch)], own)
-
-    loop(1, npatch, lambda o: lncopy(o, band).start())
     for g in gw:
         if not aligned:
             g.forward()
         g.finish()
+    norm = combined(2, 1e-06)
+    grow(band).finish()
 
     head0 = (idx * own) // HEAD_DIM
     span = nheads * HEAD_DIM
     held = pl.ds(pl.multiple_of(head0 * HEAD_DIM, HEAD_DIM), span)
-    query = (dot(qw[held, :], ln[band]) * 0.125).astype(BF16)
-
-    def score(source):
-        tokens_of = ln[source]
-        keys = dot(kw[held, :], tokens_of).astype(BF16)
-        vals[source] = dot(vw[held, :], tokens_of).astype(BF16)
+
+    def project(source):
+        projected = dot(pw[...], normalize(xr[source], norm).astype(BF16)).astype(BF16)
+        wide = projected.astype(F32)
+        wide = wide - jnp.mean(wide, axis=0, keepdims=True)
+        spread = jnp.mean(wide * wide, axis=0, keepdims=True)
+        return projected, (wide * lax.rsqrt(spread + 1e-05)).astype(BF16)
+
+    def attend(normed, query, first):
+        keys = dot(kw[held, :], normed).astype(BF16)
+        values = dot(vw[held, :], normed).astype(BF16)
         for h in range(nheads):
             part = slice(h * HEAD_DIM, (h + 1) * HEAD_DIM)
-            scores[source, h] = dot_tn(keys[part], query[part])
-
-    def relay(o):
-        lncopy(o, other(band, -o, npatch)).wait_recv()
-        gln(o).start()
-
-    score(band)
-    loop(1, npatch, relay)
-    loop(1, npatch, lambda o: gln(o).forward())
-
-    def arrive(o):
-        gln(o).finish()
-        score(other(band, -o, npatch))
-
-    loop(1, npatch, arrive)
-
+            scores = dot_tn(keys[part], query[part])
+            peak = jnp.max(scores, axis=0, keepdims=True)
+            if not first:
+                old = peaks[h]
+                peak = jnp.maximum(peak, old)
+                factor = jnp.exp(old - peak)
+            weights = jnp.exp(scores - peak)
+            total = jnp.sum(weights, axis=0, keepdims=True)
+            update = dot(values[part], weights.astype(BF16))
+            if not first:
+                total = total + totals[h] * factor
+                update = update + sums[part, :] * factor
+            peaks[h] = peak
+            totals[h] = total
+            sums[part, :] = update
+
+    def relay(rank):
+        source = nearest(rank)
+        zrow(source, source).wait_recv()
+        grow(source).start()
+
+    relay(1)
+    projected, normed = project(band)
+    proj[...] = projected
+    qry[...] = (dot(qw[held, :], normed) * 0.125).astype(BF16)
+    if npatch > 2:
+        relay(2)
+    grow(nearest(1)).forward()
+    attend(normed, qry[...], True)
+
+    def arrive(rank):
+        source = nearest(rank)
+        grow(source).finish()
+        attend(project(source)[1], qry[...], False)
+
+    for rank in range(1, min(npatch, 3)):
+        if rank + 2 < npatch:
+            relay(rank + 2)
+        if rank + 1 < npatch:
+            grow(nearest(rank + 1)).forward()
+        arrive(rank)
+
+    def further(rank):
+        if npatch > 4:
+            @pl.when(rank + 2 < npatch)
+            def _():
+                relay(rank + 2)
+
+            @pl.when(rank + 1 < npatch)
+            def _():
+                grow(nearest(rank + 1)).forward()
+        arrive(rank)
+
+    loop(3, npatch, further)
     for h in range(nheads):
         part = slice(h * HEAD_DIM, (h + 1) * HEAD_DIM)
-
-        def peak_of(b, peak):
-            return jnp.maximum(peak, jnp.max(scores[b, h], axis=0, keepdims=True))
-
-        def add(b, so_far):
-            total, weighted = so_far
-            weights = jnp.exp(scores[b, h] - peak)
-            total = total + jnp.sum(weights, axis=0, keepdims=True)
-            return total, weighted + dot(vals[b, part], weights.astype(BF16))
-
-        peak = jnp.full((1, tokens), -jnp.inf, F32)
-        so_far = (jnp.zeros((1, tokens), F32), jnp.zeros((HEAD_DIM, tokens), F32))
-        if npatch <= 4:
-            for b in range(npatch):
-                peak = peak_of(b, peak)
-            for b in range(npatch):
-                so_far = add(b, so_far)
-        else:
-            peak = lax.fori_loop(0, npatch, peak_of, peak)
-            so_far = lax.fori_loop(0, npatch, add, so_far)
-        attn[part, :] = (so_far[1] / so_far[0]).astype(BF16)
+        attn[part, :] = (sums[part, :] / totals[h]).astype(BF16)
 
     skip = pl.multiple_of(idx * own - head0 * HEAD_DIM, 16)
     at[mine, :] = attn[pl.ds(skip, own), :]
@@ -377,8 +400,8 @@
 
     for g in gw + gx + [gpw, gow, gat]:
         g.drain()
-    loop(1, npatch, lambda o: gln(o).drain())
-    loop(1, npatch, lambda o: lncopy(o, band).wait_send())
+    loop(0, npatch, lambda b: grow(b).drain())
+    loop(1, npatch, lambda r: zrow(nearest(r), band).wait_send())
     for layer in range(3):
         loop(1, everyone, lambda p: zcopy(layer, p).wait_send())
     for layer in range(2):
@@ -422,14 +445,16 @@
             pltpu.VMEM((own, C), BF16),
         ]
         + [pltpu.VMEM((C, C), BF16)] * 5
-        + [pltpu.VMEM((C, tokens), BF16)] * 4
+        + [pltpu.VMEM((C, tokens), BF16)] * 3
         + [
             pltpu.VMEM((3, npatch, nidx * 8, 128), F32),
             pltpu.VMEM((2, 2, own, tokens), BF16),
             pltpu.VMEM((2, 2, own, tokens), BF16),
             pltpu.VMEM((npatch, C, tokens), BF16),
-            pltpu.VMEM((npatch, span, tokens), BF16),
-            pltpu.VMEM((npatch, nheads, tokens, tokens), F32),
+            pltpu.VMEM((span, tokens), BF16),
+            pltpu.VMEM((nheads, 1, tokens), F32),
+            pltpu.VMEM((nheads, 1, tokens), F32),
+            pltpu.VMEM((span, tokens), F32),
             pltpu.VMEM((span, tokens), BF16),
             pltpu.VMEM((C, tokens), BF16),
             pltpu.VMEM((own, tokens), BF16),

time: 61.6 us -> 64.2 us (1.042)
  Pallas kernels: 58.5 us -> 61.1 us
    pallas_call x1, Pallas kernels: 58.5 us -> 61.1 us  [local(): pl.pallas_call(functools.partial(kernel, npatch, nchan, nsub, own, nheads...]
where the time goes in v3:
time: 64.2 us; the launch traced here: 64.1 us
  Pallas kernels  61.1 us (95%)
  other arithmetic  1.69 us (3%)
  between operations  0.67 us (1%)
    pallas_call x1, Pallas kernels, local(): pl.pallas_call(functools.partial(kernel, npatch, nchan, nsub, own, nheads...  61.1 us
    convert_element_type x1, other arithmetic, local(): return total.astype(BF16)  1.56 us

profile of v3, /device:TPU:1, one launch (start us, length us, event | category | flops | bytes accessed | tf_op | source)
XLA Modules:
  0.0 64.1 jit_solution(15753057286719403599)
XLA Ops:
  0.7 0.1 sine_convert_fusion
  0.7 0.1 pad_maximum_fusion
  0.8 0.6 broadcast_in_dim.2.emb
  1.4 61.1 %shard_map.109 = f32[160,256]{1,0:T(8,128)} custom-call(bf16[160,256]{1,0:T(8,128)(2,1)} %latent.1, bf16[16,320]{1,0:T(8,128)(2,1)} %broadcast_in_dim.2.emb, bf16[320,1280]{1,0:T(8,128)(2,1)} %bitcast.2, bf16[160,1280]{1,0:T(8,128)(2,1)} %time_proj.1, bf16[9,160,640]{2,1,0:T(8,128)(2,1)} %conv1_w.1, bf16[9,160,640]{2,1,0:T(8,128)(2,1)} %conv2_w.1, ...), custom_call_target="tpu_custom_call" | custom-call | tf_op jit(solution)/shard_map/pallas_call | solution.py:435
  62.5 1.6 %convert_element_type.16 = bf16[160,256]{1,0:T(8,128)(2,1)} convert(f32[160,256]{1,0:T(8,128)} %shard_map.109) | non-fusion elementwise | flops 40960 | bytes 245760 | tf_op jit(solution)/shard_map/convert_element_type | solution.py:477

commit v4 on v3

--- a/solution.py
+++ b/solution.py
@@ -20,8 +20,8 @@
 BF16 = jnp.bfloat16
 HIGH = lax.Precision.HIGHEST
 
-G_PW, G_OW, G_Q, G_K, G_V, G_X1, G_X2, G_AT = range(8)
-G_LN = 8
+G_PW, G_OW, G_Q, G_K, G_V, G_X1, G_X2, G_X3, G_AT = range(9)
+G_LN = 9
 
 
 def dot(a, b, precision=None):
@@ -53,7 +53,7 @@
     npatch, nchan, nsub, own, nheads,
     latent, emb, time_w1, time_proj, conv1_w, conv2_w, proj_in_w, q_w, kv_w, out_w, proj_out_w,
     out,
-    tw1, tpj, cw1, cw2, po, pw, ow, qw, kw, vw, x1, x2, at, zst, hsend, hrecv,
+    tw1, tpj, cw1, cw2, po, pw, ow, qw, kw, vw, x1, x2, x3, at, e16, et16, spread_w, zst, hsend, hrecv,
     xr, qry, peaks, totals, sums, attn, proj, res,
     lsem, gsend, grecv, zsend, zrecv, hssem, hrsem, lnsend, lnrecv,
 ):
@@ -70,17 +70,24 @@
 
     mine = rows(idx, own)
     pairs = [
-        (conv1_w, cw1), (time_w1, tw1), (time_proj, tpj), (q_w, qw.at[mine]),
-        (kv_w.at[0], kw.at[mine]), (kv_w.at[1], vw.at[mine]), (proj_in_w, pw.at[mine]),
-        (conv2_w, cw2), (out_w, ow.at[mine]), (proj_out_w, po),
+        (time_w1, tw1), (time_proj, tpj), (q_w, qw.at[mine]), (kv_w.at[0], kw.at[mine]),
+        (kv_w.at[1], vw.at[mine]), (proj_in_w, pw.at[mine]), (out_w, ow.at[mine]), (proj_out_w, po),
     ]
+    for held, weight in ((conv1_w, cw1), (conv2_w, cw2)):
+        for tap in range(9):
+            place = (0, 2, 1)[tap // 3]
+            part = weight.at[pl.ds(place * own, own), pl.ds(tap % 3 * C, C)]
+            pairs.append((held.at[tap], part))
     loads = [pltpu.make_async_copy(a, b, lsem.at[i]) for i, (a, b) in enumerate(pairs)]
-    L_C1, L_T1, L_TP, L_Q, L_K, L_V, L_PW, L_C2, L_OW, L_PO = loads
-    for load in loads:
+    L_T1, L_TP, L_Q, L_K, L_V, L_PW, L_OW, L_PO = loads[:8]
+    L_CONV = (loads[8:17], loads[17:26])
+    for load in loads[:2] + L_CONV[0] + loads[2:8] + L_CONV[1]:
         load.start()
 
     def other(k, by, count):
-        return lax.rem(k + by + count, count)
+        to = k + by + count
+        to = jnp.where(to >= 2 * count, to - 2 * count, to)
+        return jnp.where(to >= count, to - count, to)
 
     class Gather:
         def __init__(self, g, buf, size, only_sub=False):
@@ -124,29 +131,38 @@
         Gather(G_Q, qw, own, aligned), Gather(G_K, kw, own, aligned), Gather(G_V, vw, own, aligned),
     ]
     gpw, gow = Gather(G_PW, pw, own), Gather(G_OW, ow, own)
-    gx = [Gather(G_X1, x1, own), Gather(G_X2, x2, own)]
+    gx = [Gather(G_X1, x1, own), Gather(G_X2, x2, own), Gather(G_X3, x3, own)]
     gat = Gather(G_AT, at, own)
 
     cell = GROUP * tokens
 
-    def members(shape, group_dim, size):
+    def members(shape, group_dim, size, times=1):
         gi = lax.broadcasted_iota(jnp.int32, shape, group_dim)
         ci = lax.broadcasted_iota(jnp.int32, shape, 1 - group_dim)
+        period = shape[group_dim] // times
+        for k in range(times - 1, 0, -1):
+            gi = jnp.where(gi >= k * period, gi - k * period, gi)
         g = gi & 7
         first = (gi >> 3) * size + g * GROUP
         inside = (ci >= first) & (ci < first + GROUP) & (g < size // GROUP)
-        return jnp.where(inside, 1.0, 0.0).astype(F32)
+        return jnp.where(inside, 1.0, 0.0).astype(BF16)
 
     def stats(x, layer):
-        e = members((8, own), 0, own)
-        et = members((own, 8), 1, own)
-        mean = jnp.sum(dot(e, x, HIGH), axis=1, keepdims=True) * (1.0 / cell)
-        mean = jnp.broadcast_to(mean, (8, 128))
-        mc = dot(et, mean, HIGH)
-        dev = x - jnp.concatenate([mc] * (tokens // 128), axis=1)
-        m2 = jnp.sum(dot(e, dev * dev, HIGH), axis=1, keepdims=True)
-        lane = lax.broadcasted_iota(jnp.int32, (8, 128), 1)
-        zst[layer, band, rows(idx, 8)] = jnp.where(lane < 64, mean, m2)
+        mean = jnp.sum(dot(e16[...], x), axis=1, keepdims=True) * (1.0 / cell)
+        mean = jnp.broadcast_to(mean, (16, 128))
+        shift = mean.astype(BF16)
+        sc = dot(et16[...], shift)
+        sq = jnp.zeros((own, 128), F32)
+        for k in range(0, tokens, 128):
+            dev = x[:, k : k + 128].astype(F32) - sc
+            sq = sq + dev * dev
+        hi = sq.astype(BF16)
+        lo = (sq - hi.astype(F32)).astype(BF16)
+        m2 = jnp.sum(dot(e16[...], jnp.concatenate([hi, lo], axis=1)), axis=1, keepdims=True)
+        gap = mean - shift.astype(F32)
+        m2 = jnp.maximum(m2 - cell * (gap * gap), 0.0)
+        lane = lax.broadcasted_iota(jnp.int32, (16, 128), 1)
+        zst[layer, band, rows(idx, 8)] = jnp.where(lane < 64, mean, m2)[0:8]
 
     everyone = npatch * nidx
 
@@ -181,7 +197,11 @@
         pair = jnp.where(
             lane < 64, jnp.broadcast_to(mean, shape), jnp.broadcast_to(lax.rsqrt(var + eps), shape)
         )
-        return dot(members((C, nidx * 8), 1, own), pair, HIGH)
+        one = pair.astype(BF16)
+        rest = pair - one.astype(F32)
+        two = rest.astype(BF16)
+        three = (rest - two.astype(F32)).astype(BF16)
+        return dot(spread_w[...], jnp.concatenate([one, two, three], axis=0))
 
     def normalize(x, both):
         return (x.astype(F32) - both[:, 0:1]) * both[:, 64:65]
@@ -197,28 +217,24 @@
 
     def convolve(act, weight, layer):
         col = lax.broadcasted_iota(jnp.int32, act.shape, 1)
-        taps = [
+        taps = jnp.concatenate([
             jnp.where(col == 0, 0.0, pltpu.roll(act, 1, 1)).astype(BF16),
             act.astype(BF16),
             jnp.where(col == tokens - 1, 0.0, pltpu.roll(act, tokens - 1, 1)).astype(BF16),
-        ]
-
-        def row(i):
-            return sum(dot(weight[3 * i + j], taps[j]) for j in range(3))
-
-        hsend[layer, 0] = row(0).astype(BF16)
+        ], axis=0)
+        outer = dot(weight[0 : 2 * own, :], taps).astype(BF16)
+        hsend[layer, 0] = outer[0:own]
+        hsend[layer, 1] = outer[own : 2 * own]
 
         @pl.when(has_below)
         def _():
             hcopy(layer, 0).start()
 
-        hsend[layer, 1] = row(2).astype(BF16)
-
         @pl.when(has_above)
         def _():
             hcopy(layer, 1).start()
 
-        return row(1)
+        return dot(weight[2 * own : 3 * own, :], taps)
 
     def neighbours(layer):
         @pl.when(has_above)
@@ -245,7 +261,10 @@
         barrier, inc=1, device_id=peer(p, 1), device_id_type=MESH))
     x1[mine, :] = latent[...]
     lat = latent[...].astype(F32)
-    stats(lat, 0)
+    e16[...] = members((16, own), 0, own)
+    et16[...] = members((own, 16), 1, own)
+    stats(latent[...], 0)
+    spread_w[...] = members(spread_w.shape, 1, own, 3)
 
     pl.semaphore_wait(barrier, everyone - 1)
 
@@ -263,11 +282,12 @@
     gx[0].finish()
     L_PW.wait()
     gpw.start()
-    L_C1.wait()
+    for load in L_CONV[0]:
+        load.wait()
     centre = convolve(silu(normalize(x1[...], norm)), cw1, 0)
     conv_one = (centre + neighbours(0) + bias[:, 0:1]).astype(BF16)
     x2[mine, :] = conv_one
-    stats(conv_one.astype(F32), 1)
+    stats(conv_one, 1)
 
     share(1)
     gx[1].start()
@@ -277,11 +297,13 @@
     gx[1].finish()
     L_OW.wait()
     gow.start()
-    L_C2.wait()
+    for load in L_CONV[1]:
+        load.wait()
     centre = convolve(silu(normalize(x2[...], norm)), cw2, 1)
     resnet = (lat + (centre + neighbours(1))).astype(BF16)
     res[...] = resnet
-    xr[band, mine, :] = resnet
+    x3[mine, :] = resnet
+    stats(resnet, 2)
 
     def zrow(to, source):
         ref = xr.at[source, mine]
@@ -300,30 +322,29 @@
         beyond = jnp.where(2 * band < npatch - 1, rank, npatch - 1 - rank)
         return jnp.where(rank <= 2 * near, band + (1 - 2 * odd) * step, beyond)
 
-    grow(band).start()
-    loop(1, npatch, lambda r: zrow(nearest(r), band).start())
-    stats(resnet.astype(F32), 2)
     share(2)
-    grow(band).forward()
+    gx[2].start()
     gow.forward()
+    gx[2].forward()
     gpw.finish()
     for g in gw:
         if not aligned:
             g.forward()
         g.finish()
     norm = combined(2, 1e-06)
-    grow(band).finish()
+    gx[2].finish()
 
     head0 = (idx * own) // HEAD_DIM
     span = nheads * HEAD_DIM
     held = pl.ds(pl.multiple_of(head0 * HEAD_DIM, HEAD_DIM), span)
 
-    def project(source):
-        projected = dot(pw[...], normalize(xr[source], norm).astype(BF16)).astype(BF16)
-        wide = projected.astype(F32)
-        wide = wide - jnp.mean(wide, axis=0, keepdims=True)
-        spread = jnp.mean(wide * wide, axis=0, keepdims=True)
-        return projected, (wide * lax.rsqrt(spread + 1e-05)).astype(BF16)
+    projected = dot(pw[...], normalize(x3[...], norm).astype(BF16)).astype(BF16)
+    proj[...] = projected
+    wide = projected.astype(F32)
+    wide = wide - jnp.mean(wide, axis=0, keepdims=True)
+    spread = jnp.mean(wide * wide, axis=0, keepdims=True)
+    xr[band] = (wide * lax.rsqrt(spread + 1e-05)).astype(BF16)
+    loop(1, npatch, lambda r: zrow(nearest(r), band).start())
 
     def attend(normed, query, first):
         keys = dot(kw[held, :], normed).astype(BF16)
@@ -351,19 +372,17 @@
         zrow(source, source).wait_recv()
         grow(source).start()
 
+    qry[...] = (dot(qw[held, :], xr[band]) * 0.125).astype(BF16)
     relay(1)
-    projected, normed = project(band)
-    proj[...] = projected
-    qry[...] = (dot(qw[held, :], normed) * 0.125).astype(BF16)
+    attend(xr[band], qry[...], True)
     if npatch > 2:
         relay(2)
     grow(nearest(1)).forward()
-    attend(normed, qry[...], True)
 
     def arrive(rank):
         source = nearest(rank)
         grow(source).finish()
-        attend(project(source)[1], qry[...], False)
+        attend(xr[source], qry[...], False)
 
     for rank in range(1, min(npatch, 3)):
         if rank + 2 < npatch:
@@ -400,7 +419,7 @@
 
     for g in gw + gx + [gpw, gow, gat]:
         g.drain()
-    loop(0, npatch, lambda b: grow(b).drain())
+    loop(1, npatch, lambda r: grow(nearest(r)).drain())
     loop(1, npatch, lambda r: zrow(nearest(r), band).wait_send())
     for layer in range(3):
         loop(1, everyone, lambda p: zcopy(layer, p).wait_send())
@@ -423,10 +442,11 @@
     nidx = nchan * nsub
     temb = time_w1.shape[0]
     half_width = FREQ // 2
-    frequency = jnp.exp(-math.log(10000.0) * jnp.arange(half_width, dtype=F32) / half_width)
-    angles = timestep[0].astype(F32) * frequency
-    embedded = jnp.concatenate([jnp.cos(angles), jnp.sin(angles)]).astype(BF16)
-    emb = jnp.broadcast_to(embedded[None, :], (16, FREQ))
+    place = lax.broadcasted_iota(jnp.int32, (16, FREQ), 1)
+    first = place < half_width
+    order = jnp.where(first, place, place - half_width).astype(F32)
+    angles = timestep[0].astype(F32) * jnp.exp(-math.log(10000.0) * order / half_width)
+    emb = jnp.where(first, jnp.cos(angles), jnp.sin(angles)).astype(BF16)
     vmem = pl.BlockSpec(memory_space=pltpu.VMEM)
     hbm = pl.BlockSpec(memory_space=pl.ANY)
     dma = pltpu.SemaphoreType.DMA
@@ -440,12 +460,17 @@
         scratch_shapes=[
             pltpu.VMEM((FREQ, temb), BF16),
             pltpu.VMEM((own, temb), BF16),
-            pltpu.VMEM((9, own, C), BF16),
-            pltpu.VMEM((9, own, C), BF16),
+            pltpu.VMEM((3 * own, 3 * C), BF16),
+            pltpu.VMEM((3 * own, 3 * C), BF16),
             pltpu.VMEM((own, C), BF16),
         ]
         + [pltpu.VMEM((C, C), BF16)] * 5
-        + [pltpu.VMEM((C, tokens), BF16)] * 3
+        + [pltpu.VMEM((C, tokens), BF16)] * 4
+        + [
+            pltpu.VMEM((16, own), BF16),
+            pltpu.VMEM((own, 16), BF16),
+            pltpu.VMEM((C, 3 * nidx * 8), BF16),
+        ]
         + [
             pltpu.VMEM((3, npatch, nidx * 8, 128), F32),
             pltpu.VMEM((2, 2, own, tokens), BF16),
@@ -458,7 +483,7 @@
             pltpu.VMEM((span, tokens), BF16),
             pltpu.VMEM((C, tokens), BF16),
             pltpu.VMEM((own, tokens), BF16),
-            dma((10,)),
+            dma((26,)),
             dma((ngather, nchan, nsub)),
             dma((ngather, nchan, nsub)),
             dma((3, npatch * nidx)),

time: 64.2 us -> 64.8 us (level)
    convert_element_type x0 -> x1, other arithmetic: none -> 0.68 us  [local(): emb = jnp.where(first, jnp.cos(angles), jnp.sin(angles)).astype(BF16)]
where the time goes in v4:
time: 64.8 us; the launch traced here: 64.7 us
  Pallas kernels  61.7 us (95%)
  other arithmetic  2.25 us (3%)
  between operations  0.67 us (1%)
    pallas_call x1, Pallas kernels, local(): pl.pallas_call(functools.partial(kernel, npatch, nchan, nsub, own, nheads...  61.7 us
    convert_element_type x1, other arithmetic, local(): return total.astype(BF16)  1.56 us

profile of v4, /device:TPU:1, one launch (start us, length us, event | category | flops | bytes accessed | tf_op | source)
XLA Modules:
  0.0 64.7 jit_solution(6066355749201083554)
XLA Ops:
  0.7 0.7 %select_convert_fusion.emb = bf16[16,320]{1,0:T(8,128)(2,1)} fusion(s32[320]{0:T(512)S(1)} %iota_add_fusion, f32[]{:T(128)} %bitcast, pred[320]{0:T(512)(128)(4,1)S(1)} %iota_compare_fusion), kind=kLoop, calls=%fused_computation | loop fusion | flops 30720 | bytes 11844 | tf_op jit(solution)/shard_map/convert_element_type | solution.py:449
  1.4 61.7 %shard_map.109 = f32[160,256]{1,0:T(8,128)} custom-call(bf16[160,256]{1,0:T(8,128)(2,1)} %latent.1, bf16[16,320]{1,0:T(8,128)(2,1)} %select_convert_fusion.emb, bf16[320,1280]{1,0:T(8,128)(2,1)} %bitcast.2, bf16[160,1280]{1,0:T(8,128)(2,1)} %time_proj.1, bf16[9,160,640]{2,1,0:T(8,128)(2,1)} %conv1_w.1, bf16[9,160,640]{2,1,0:T(8,128)(2,1)} %conv2_w.1, ...), custom_call_target="tpu_custom_call" | custom-call | tf_op jit(solution)/shard_map/pallas_call | solution.py:455
  63.1 1.6 %convert_element_type.19 = bf16[160,256]{1,0:T(8,128)(2,1)} convert(f32[160,256]{1,0:T(8,128)} %shard_map.109) | non-fusion elementwise | flops 40960 | bytes 245760 | tf_op jit(solution)/shard_map/convert_element_type | solution.py:502
  (2 shorter events, 0.0 us)

commit v5 on v4

--- a/solution.py
+++ b/solution.py
@@ -51,10 +51,10 @@
 
 def kernel(
     npatch, nchan, nsub, own, nheads,
-    latent, emb, time_w1, time_proj, conv1_w, conv2_w, proj_in_w, q_w, kv_w, out_w, proj_out_w,
+    latent_hbm, emb_hbm, time_w1, time_proj, conv1_w, conv2_w, proj_in_w, q_w, kv_w, out_w, proj_out_w,
     out,
-    tw1, tpj, cw1, cw2, po, pw, ow, qw, kw, vw, x1, x2, x3, at, e16, et16, spread_w, zst, hsend, hrecv,
-    xr, qry, peaks, totals, sums, attn, proj, res,
+    emb, tw1, tpj, cw1, cw2, po, pw, ow, qw, kw, vw, x1, x2, x3, at, e16, et16, spread_w, zst, hsend, hrecv,
+    xr, vals, scores, attn, proj, res,
     lsem, gsend, grecv, zsend, zrecv, hssem, hrsem, lnsend, lnrecv,
 ):
     band = lax.axis_index("patch")
@@ -62,7 +62,7 @@
     sub = lax.axis_index("sub")
     idx = chan * nsub + sub
     nidx = nchan * nsub
-    tokens = latent.shape[1]
+    tokens = x1.shape[1]
     aligned = (own * nsub) % HEAD_DIM == 0
 
     def rows(block, size):
@@ -73,15 +73,11 @@
         (time_w1, tw1), (time_proj, tpj), (q_w, qw.at[mine]), (kv_w.at[0], kw.at[mine]),
         (kv_w.at[1], vw.at[mine]), (proj_in_w, pw.at[mine]), (out_w, ow.at[mine]), (proj_out_w, po),
     ]
-    for held, weight in ((conv1_w, cw1), (conv2_w, cw2)):
-        for tap in range(9):
-            place = (0, 2, 1)[tap // 3]
-            part = weight.at[pl.ds(place * own, own), pl.ds(tap % 3 * C, C)]
-            pairs.append((held.at[tap], part))
+    pairs += [(conv1_w, cw1), (conv2_w, cw2), (latent_hbm, x1.at[mine]), (emb_hbm, emb)]
     loads = [pltpu.make_async_copy(a, b, lsem.at[i]) for i, (a, b) in enumerate(pairs)]
     L_T1, L_TP, L_Q, L_K, L_V, L_PW, L_OW, L_PO = loads[:8]
-    L_CONV = (loads[8:17], loads[17:26])
-    for load in loads[:2] + L_CONV[0] + loads[2:8] + L_CONV[1]:
+    L_C1, L_C2, L_X, L_E = loads[8:]
+    for load in (L_X, L_E, L_T1, L_TP, L_C1, L_Q, L_K, L_V, L_PW, L_C2, L_OW, L_PO):
         load.start()
 
     def other(k, by, count):
@@ -217,24 +213,28 @@
 
     def convolve(act, weight, layer):
         col = lax.broadcasted_iota(jnp.int32, act.shape, 1)
-        taps = jnp.concatenate([
+        taps = [
             jnp.where(col == 0, 0.0, pltpu.roll(act, 1, 1)).astype(BF16),
             act.astype(BF16),
             jnp.where(col == tokens - 1, 0.0, pltpu.roll(act, tokens - 1, 1)).astype(BF16),
-        ], axis=0)
-        outer = dot(weight[0 : 2 * own, :], taps).astype(BF16)
-        hsend[layer, 0] = outer[0:own]
-        hsend[layer, 1] = outer[own : 2 * own]
+        ]
+
+        def row(i):
+            return sum(dot(weight[3 * i + j], taps[j]) for j in range(3))
+
+        hsend[layer, 0] = row(0).astype(BF16)
 
         @pl.when(has_below)
         def _():
             hcopy(layer, 0).start()
 
+        hsend[layer, 1] = row(2).astype(BF16)
+
         @pl.when(has_above)
         def _():
             hcopy(layer, 1).start()
 
-        return dot(weight[2 * own : 3 * own, :], taps)
+        return row(1)
 
     def neighbours(layer):
         @pl.when(has_above)
@@ -259,11 +259,10 @@
     barrier = pltpu.get_barrier_semaphore()
     loop(1, everyone, lambda p: pl.semaphore_signal(
         barrier, inc=1, device_id=peer(p, 1), device_id_type=MESH))
-    x1[mine, :] = latent[...]
-    lat = latent[...].astype(F32)
     e16[...] = members((16, own), 0, own)
     et16[...] = members((own, 16), 1, own)
-    stats(latent[...], 0)
+    L_X.wait()
+    stats(x1[mine, :], 0)
     spread_w[...] = members(spread_w.shape, 1, own, 3)
 
     pl.semaphore_wait(barrier, everyone - 1)
@@ -271,6 +270,7 @@
     share(0)
     gx[0].start()
     L_T1.wait()
+    L_E.wait()
     hidden = silu(dot(emb[...], tw1[...]))
     L_TP.wait()
     bias = dot_nt(tpj[...], silu(hidden).astype(BF16))
@@ -282,8 +282,7 @@
     gx[0].finish()
     L_PW.wait()
     gpw.start()
-    for load in L_CONV[0]:
-        load.wait()
+    L_C1.wait()
     centre = convolve(silu(normalize(x1[...], norm)), cw1, 0)
     conv_one = (centre + neighbours(0) + bias[:, 0:1]).astype(BF16)
     x2[mine, :] = conv_one
@@ -297,10 +296,9 @@
     gx[1].finish()
     L_OW.wait()
     gow.start()
-    for load in L_CONV[1]:
-        load.wait()
+    L_C2.wait()
     centre = convolve(silu(normalize(x2[...], norm)), cw2, 1)
-    resnet = (lat + (centre + neighbours(1))).astype(BF16)
+    resnet = (x1[mine, :].astype(F32) + (centre + neighbours(1))).astype(BF16)
     res[...] = resnet
     x3[mine, :] = resnet
     stats(resnet, 2)
@@ -346,66 +344,60 @@
     xr[band] = (wide * lax.rsqrt(spread + 1e-05)).astype(BF16)
     loop(1, npatch, lambda r: zrow(nearest(r), band).start())
 
-    def attend(normed, query, first):
+    def score(source):
+        normed = xr[source]
         keys = dot(kw[held, :], normed).astype(BF16)
-        values = dot(vw[held, :], normed).astype(BF16)
+        vals[source] = dot(vw[held, :], normed).astype(BF16)
         for h in range(nheads):
             part = slice(h * HEAD_DIM, (h + 1) * HEAD_DIM)
-            scores = dot_tn(keys[part], query[part])
-            peak = jnp.max(scores, axis=0, keepdims=True)
-            if not first:
-                old = peaks[h]
-                peak = jnp.maximum(peak, old)
-                factor = jnp.exp(old - peak)
-            weights = jnp.exp(scores - peak)
-            total = jnp.sum(weights, axis=0, keepdims=True)
-            update = dot(values[part], weights.astype(BF16))
-            if not first:
-                total = total + totals[h] * factor
-                update = update + sums[part, :] * factor
-            peaks[h] = peak
-            totals[h] = total
-            sums[part, :] = update
+            scores[source, h] = dot_tn(keys[part], query[part])
 
     def relay(rank):
         source = nearest(rank)
         zrow(source, source).wait_recv()
         grow(source).start()
 
-    qry[...] = (dot(qw[held, :], xr[band]) * 0.125).astype(BF16)
+    query = (dot(qw[held, :], xr[band]) * 0.125).astype(BF16)
+    score(band)
     relay(1)
-    attend(xr[band], qry[...], True)
-    if npatch > 2:
-        relay(2)
-    grow(nearest(1)).forward()
+
+    def pass_on(rank):
+        relay(rank)
+        grow(nearest(rank - 1)).forward()
+
+    loop(2, npatch, pass_on)
+    grow(nearest(npatch - 1)).forward()
 
     def arrive(rank):
         source = nearest(rank)
         grow(source).finish()
-        attend(xr[source], qry[...], False)
-
-    for rank in range(1, min(npatch, 3)):
-        if rank + 2 < npatch:
-            relay(rank + 2)
-        if rank + 1 < npatch:
-            grow(nearest(rank + 1)).forward()
-        arrive(rank)
-
-    def further(rank):
-        if npatch > 4:
-            @pl.when(rank + 2 < npatch)
-            def _():
-                relay(rank + 2)
-
-            @pl.when(rank + 1 < npatch)
-            def _():
-                grow(nearest(rank + 1)).forward()
-        arrive(rank)
-
-    loop(3, npatch, further)
+        score(source)
+
+    loop(1, npatch, arrive)
+
     for h in range(nheads):
         part = slice(h * HEAD_DIM, (h + 1) * HEAD_DIM)
-        attn[part, :] = (sums[part, :] / totals[h]).astype(BF16)
+
+        def peak_of(b, peak):
+            return jnp.maximum(peak, jnp.max(scores[b, h], axis=0, keepdims=True))
+
+        def add(b, so_far):
+            total, weighted = so_far
+            weights = jnp.exp(scores[b, h] - peak)
+            total = total + jnp.sum(weights, axis=0, keepdims=True)
+            return total, weighted + dot(vals[b, part], weights.astype(BF16))
+
+        peak = jnp.full((1, tokens), -jnp.inf, F32)
+        so_far = (jnp.zeros((1, tokens), F32), jnp.zeros((HEAD_DIM, tokens), F32))
+        if npatch <= 4:
+            for b in range(npatch):
+                peak = peak_of(b, peak)
+            for b in range(npatch):
+                so_far = add(b, so_far)
+        else:
+            peak = lax.fori_loop(0, npatch, peak_of, peak)
+            so_far = lax.fori_loop(0, npatch, add, so_far)
+        attn[part, :] = (so_far[1] / so_far[0]).astype(BF16)
 
     skip = pl.multiple_of(idx * own - head0 * HEAD_DIM, 16)
     at[mine, :] = attn[pl.ds(skip, own), :]
@@ -454,14 +446,15 @@
     ngather = G_LN + npatch
     total = pl.pallas_call(
         functools.partial(kernel, npatch, nchan, nsub, own, nheads),
-        out_shape=jax.ShapeDtypeStruct((own, tokens), F32),
-        in_specs=[vmem, vmem] + [hbm] * 9,
+        out_shape=pltpu.VMEM((own, tokens), F32),
+        in_specs=[hbm] * 11,
         out_specs=vmem,
         scratch_shapes=[
+            pltpu.VMEM((16, FREQ), BF16),
             pltpu.VMEM((FREQ, temb), BF16),
             pltpu.VMEM((own, temb), BF16),
-            pltpu.VMEM((3 * own, 3 * C), BF16),
-            pltpu.VMEM((3 * own, 3 * C), BF16),
+            pltpu.VMEM((9, own, C), BF16),
+            pltpu.VMEM((9, own, C), BF16),
             pltpu.VMEM((own, C), BF16),
         ]
         + [pltpu.VMEM((C, C), BF16)] * 5
@@ -476,14 +469,12 @@
             pltpu.VMEM((2, 2, own, tokens), BF16),
             pltpu.VMEM((2, 2, own, tokens), BF16),
             pltpu.VMEM((npatch, C, tokens), BF16),
-            pltpu.VMEM((span, tokens), BF16),
-            pltpu.VMEM((nheads, 1, tokens), F32),
-            pltpu.VMEM((nheads, 1, tokens), F32),
-            pltpu.VMEM((span, tokens), F32),
+            pltpu.VMEM((npatch, span, tokens), BF16),
+            pltpu.VMEM((npatch, nheads, tokens, tokens), F32),
             pltpu.VMEM((span, tokens), BF16),
             pltpu.VMEM((C, tokens), BF16),
             pltpu.VMEM((own, tokens), BF16),
-            dma((26,)),
+            dma((12,)),
             dma((ngather, nchan, nsub)),
             dma((ngather, nchan, nsub)),
             dma((3, npatch * nidx)),

time: 64.8 us -> 60.4 us (0.932)
  Pallas kernels: 61.7 us -> 58.2 us
  other arithmetic: 2.25 us -> 1.33 us
    pallas_call x1, Pallas kernels: 61.7 us -> 58.2 us  [local(): pl.pallas_call(functools.partial(kernel, npatch, nchan, nsub, own, nheads...]
    convert_element_type x1, other arithmetic: 1.56 us -> 0.65 us  [local(): return total.astype(BF16)]
where the time goes in v5:
time: 60.4 us; the launch traced here: 60.2 us
  Pallas kernels  58.2 us (96%)
  other arithmetic  1.33 us (2%)
  between operations  0.67 us (1%)
    pallas_call x1, Pallas kernels, local(): pl.pallas_call(functools.partial(kernel, npatch, nchan, nsub, own, nheads...  58.2 us

profile of v5, /device:TPU:1, one launch (start us, length us, event | category | flops | bytes accessed | tf_op | source)
XLA Modules:
  0.0 60.2 jit_solution(15490897864232044019)
XLA Ops:
  0.7 0.7 %select_convert_fusion.emb_hbm = bf16[16,320]{1,0:T(8,128)(2,1)} fusion(s32[320]{0:T(512)S(1)} %iota_add_fusion, f32[]{:T(128)} %bitcast, pred[320]{0:T(512)(128)(4,1)S(1)} %iota_compare_fusion), kind=kLoop, calls=%fused_computation | loop fusion | flops 30720 | bytes 11844 | tf_op jit(solution)/shard_map/convert_element_type | solution.py:441
  1.4 58.2 %shard_map.109 = f32[160,256]{1,0:T(8,128)S(1)} custom-call(bf16[160,256]{1,0:T(8,128)(2,1)} %latent_hbm.1, bf16[16,320]{1,0:T(8,128)(2,1)} %select_convert_fusion.emb_hbm, bf16[320,1280]{1,0:T(8,128)(2,1)} %bitcast.2, bf16[160,1280]{1,0:T(8,128)(2,1)} %time_proj.1, bf16[9,160,640]{2,1,0:T(8,128)(2,1)} %conv1_w.1, bf16[9,160,640]{2,1,0:T(8,128)(2,1)} %conv2_w.1, ...), custom_call_target="tpu_custom_call" | custom-call | tf_op jit(solution)/shard_map/pallas_call | solution.py:447
  59.6 0.6 %convert_element_type.19 = bf16[160,256]{1,0:T(8,128)(2,1)} convert(f32[160,256]{1,0:T(8,128)S(1)} %shard_map.109) | non-fusion elementwise | flops 40960 | bytes 245760 | tf_op jit(solution)/shard_map/convert_element_type | solution.py:493
  (2 shorter events, 0.0 us)

commit v6 on v5

--- a/solution.py
+++ b/solution.py
@@ -20,8 +20,8 @@
 BF16 = jnp.bfloat16
 HIGH = lax.Precision.HIGHEST
 
-G_PW, G_OW, G_Q, G_K, G_V, G_X1, G_X2, G_X3, G_AT = range(9)
-G_LN = 9
+G_PW, G_OW, G_Q, G_K, G_V, G_X1, G_X2, G_AT = range(8)
+G_LN = 8
 
 
 def dot(a, b, precision=None):
@@ -53,7 +53,7 @@
     npatch, nchan, nsub, own, nheads,
     latent_hbm, emb_hbm, time_w1, time_proj, conv1_w, conv2_w, proj_in_w, q_w, kv_w, out_w, proj_out_w,
     out,
-    emb, tw1, tpj, cw1, cw2, po, pw, ow, qw, kw, vw, x1, x2, x3, at, e16, et16, spread_w, zst, hsend, hrecv,
+    emb, tw1, tpj, cw1, cw2, po, pw, ow, qw, kw, vw, x1, x2, nmean, nscale, at, e16, et16, spread_w, zst, hsend, hrecv,
     xr, vals, scores, attn, proj, res,
     lsem, gsend, grecv, zsend, zrecv, hssem, hrsem, lnsend, lnrecv,
 ):
@@ -127,7 +127,7 @@
         Gather(G_Q, qw, own, aligned), Gather(G_K, kw, own, aligned), Gather(G_V, vw, own, aligned),
     ]
     gpw, gow = Gather(G_PW, pw, own), Gather(G_OW, ow, own)
-    gx = [Gather(G_X1, x1, own), Gather(G_X2, x2, own), Gather(G_X3, x3, own)]
+    gx = [Gather(G_X1, x1, own), Gather(G_X2, x2, own)]
     gat = Gather(G_AT, at, own)
 
     cell = GROUP * tokens
@@ -300,8 +300,7 @@
     centre = convolve(silu(normalize(x2[...], norm)), cw2, 1)
     resnet = (x1[mine, :].astype(F32) + (centre + neighbours(1))).astype(BF16)
     res[...] = resnet
-    x3[mine, :] = resnet
-    stats(resnet, 2)
+    xr[band, mine, :] = resnet
 
     def zrow(to, source):
         ref = xr.at[source, mine]
@@ -320,60 +319,75 @@
         beyond = jnp.where(2 * band < npatch - 1, rank, npatch - 1 - rank)
         return jnp.where(rank <= 2 * near, band + (1 - 2 * odd) * step, beyond)
 
+    loop(1, npatch, lambda r: zrow(nearest(r), band).start())
+    grow(band).start()
+    stats(resnet, 2)
     share(2)
-    gx[2].start()
+    grow(band).forward()
+
+    def relay(rank):
+        source = nearest(rank)
+        zrow(source, source).wait_recv()
+        grow(source).start()
+
     gow.forward()
-    gx[2].forward()
     gpw.finish()
     for g in gw:
         if not aligned:
             g.forward()
         g.finish()
+    relay(1)
     norm = combined(2, 1e-06)
-    gx[2].finish()
+    nmean[...] = jnp.broadcast_to(norm[:, 0:1], (C, 128))
+    nscale[...] = jnp.broadcast_to(norm[:, 64:65], (C, 128))
+    if npatch > 2:
+        relay(2)
+    grow(nearest(1)).forward()
+    grow(band).finish()
 
     head0 = (idx * own) // HEAD_DIM
     span = nheads * HEAD_DIM
     held = pl.ds(pl.multiple_of(head0 * HEAD_DIM, HEAD_DIM), span)
 
-    projected = dot(pw[...], normalize(x3[...], norm).astype(BF16)).astype(BF16)
-    proj[...] = projected
-    wide = projected.astype(F32)
-    wide = wide - jnp.mean(wide, axis=0, keepdims=True)
-    spread = jnp.mean(wide * wide, axis=0, keepdims=True)
-    xr[band] = (wide * lax.rsqrt(spread + 1e-05)).astype(BF16)
-    loop(1, npatch, lambda r: zrow(nearest(r), band).start())
-
-    def score(source):
-        normed = xr[source]
+    def project(source):
+        halves = [
+            (xr[source, :, k : k + 128].astype(F32) - nmean[...]) * nscale[...]
+            for k in range(0, tokens, 128)
+        ]
+        normed = jnp.concatenate(halves, axis=1).astype(BF16)
+        projected = dot(pw[...], normed).astype(BF16)
+        wide = projected.astype(F32)
+        wide = wide - jnp.mean(wide, axis=0, keepdims=True)
+        spread = jnp.mean(wide * wide, axis=0, keepdims=True)
+        return projected, (wide * lax.rsqrt(spread + 1e-05)).astype(BF16)
+
+    def score(source, normed):
         keys = dot(kw[held, :], normed).astype(BF16)
         vals[source] = dot(vw[held, :], normed).astype(BF16)
         for h in range(nheads):
             part = slice(h * HEAD_DIM, (h + 1) * HEAD_DIM)
             scores[source, h] = dot_tn(keys[part], query[part])
 
-    def relay(rank):
-        source = nearest(rank)
-        zrow(source, source).wait_recv()
-        grow(source).start()
-
-    query = (dot(qw[held, :], xr[band]) * 0.125).astype(BF16)
-    score(band)
-    relay(1)
-
-    def pass_on(rank):
-        relay(rank)
-        grow(nearest(rank - 1)).forward()
-
-    loop(2, npatch, pass_on)
-    grow(nearest(npatch - 1)).forward()
+    projected, normed = project(band)
+    proj[...] = projected
+    query = (dot(qw[held, :], normed) * 0.125).astype(BF16)
+    score(band, normed)
 
     def arrive(rank):
         source = nearest(rank)
         grow(source).finish()
-        score(source)
-
-    loop(1, npatch, arrive)
+        score(source, project(source)[1])
+
+    def step(rank):
+        relay(rank + 2)
+        grow(nearest(rank + 1)).forward()
+        arrive(rank)
+
+    loop(1, npatch - 2, step)
+    if npatch > 2:
+        grow(nearest(npatch - 1)).forward()
+        arrive(npatch - 2)
+    arrive(npatch - 1)
 
     for h in range(nheads):
         part = slice(h * HEAD_DIM, (h + 1) * HEAD_DIM)
@@ -411,7 +425,7 @@
 
     for g in gw + gx + [gpw, gow, gat]:
         g.drain()
-    loop(1, npatch, lambda r: grow(nearest(r)).drain())
+    loop(0, npatch, lambda b: grow(b).drain())
     loop(1, npatch, lambda r: zrow(nearest(r), band).wait_send())
     for layer in range(3):
         loop(1, everyone, lambda p: zcopy(layer, p).wait_send())
@@ -458,8 +472,10 @@
             pltpu.VMEM((own, C), BF16),
         ]
         + [pltpu.VMEM((C, C), BF16)] * 5
-        + [pltpu.VMEM((C, tokens), BF16)] * 4
+        + [pltpu.VMEM((C, tokens), BF16)] * 2
+        + [pltpu.VMEM((C, 128), F32)] * 2
         + [
+            pltpu.VMEM((C, tokens), BF16),
             pltpu.VMEM((16, own), BF16),
             pltpu.VMEM((own, 16), BF16),
             pltpu.VMEM((C, 3 * nidx * 8), BF16),

time: 60.4 us -> 56.7 us (0.939)
  Pallas kernels: 58.2 us -> 54.5 us
    pallas_call x1, Pallas kernels: 58.2 us -> 54.5 us  [local(): pl.pallas_call(functools.partial(kernel, npatch, nchan, nsub, own, nheads...]
where the time goes in v6:
time: 56.7 us; the launch traced here: 56.5 us
  Pallas kernels  54.5 us (96%)
  other arithmetic  1.33 us (2%)
  between operations  0.67 us (1%)
    pallas_call x1, Pallas kernels, local(): pl.pallas_call(functools.partial(kernel, npatch, nchan, nsub, own, nheads...  54.5 us

profile of v6, /device:TPU:1, one launch (start us, length us, event | category | flops | bytes accessed | tf_op | source)
XLA Modules:
  0.0 56.5 jit_solution(4921212450393738095)
XLA Ops:
  0.7 0.7 %select_convert_fusion.emb_hbm = bf16[16,320]{1,0:T(8,128)(2,1)} fusion(s32[320]{0:T(512)S(1)} %iota_add_fusion, f32[]{:T(128)} %bitcast, pred[320]{0:T(512)(128)(4,1)S(1)} %iota_compare_fusion), kind=kLoop, calls=%fused_computation | loop fusion | flops 30720 | bytes 11844 | tf_op jit(solution)/shard_map/convert_element_type | solution.py:455
  1.4 54.5 %shard_map.109 = f32[160,256]{1,0:T(8,128)S(1)} custom-call(bf16[160,256]{1,0:T(8,128)(2,1)} %latent_hbm.1, bf16[16,320]{1,0:T(8,128)(2,1)} %select_convert_fusion.emb_hbm, bf16[320,1280]{1,0:T(8,128)(2,1)} %bitcast.2, bf16[160,1280]{1,0:T(8,128)(2,1)} %time_proj.1, bf16[9,160,640]{2,1,0:T(8,128)(2,1)} %conv1_w.1, bf16[9,160,640]{2,1,0:T(8,128)(2,1)} %conv2_w.1, ...), custom_call_target="tpu_custom_call" | custom-call | tf_op jit(solution)/shard_map/pallas_call | solution.py:461
  55.9 0.6 %convert_element_type.19 = bf16[160,256]{1,0:T(8,128)(2,1)} convert(f32[160,256]{1,0:T(8,128)S(1)} %shard_map.109) | non-fusion elementwise | flops 40960 | bytes 245760 | tf_op jit(solution)/shard_map/convert_element_type | solution.py:509
  (2 shorter events, 0.0 us)

commit v7 on v6

--- a/solution.py
+++ b/solution.py
@@ -51,10 +51,10 @@
 
 def kernel(
     npatch, nchan, nsub, own, nheads,
-    latent_hbm, emb_hbm, time_w1, time_proj, conv1_w, conv2_w, proj_in_w, q_w, kv_w, out_w, proj_out_w,
+    latent_hbm, timestep, time_w1, time_proj, conv1_w, conv2_w, proj_in_w, q_w, kv_w, out_w, proj_out_w,
     out,
-    emb, tw1, tpj, cw1, cw2, po, pw, ow, qw, kw, vw, x1, x2, nmean, nscale, at, e16, et16, spread_w, zst, hsend, hrecv,
-    xr, vals, scores, attn, proj, res,
+    tw1, tpj, cw1, cw2, po, pw, ow, qw, kw, vw, x1, x2, nmean, nscale, at, e16, et16, spread_w, zst, hsend, hrecv,
+    xr, vals, scores, peaks, attn, proj, res,
     lsem, gsend, grecv, zsend, zrecv, hssem, hrsem, lnsend, lnrecv,
 ):
     band = lax.axis_index("patch")
@@ -73,11 +73,11 @@
         (time_w1, tw1), (time_proj, tpj), (q_w, qw.at[mine]), (kv_w.at[0], kw.at[mine]),
         (kv_w.at[1], vw.at[mine]), (proj_in_w, pw.at[mine]), (out_w, ow.at[mine]), (proj_out_w, po),
     ]
-    pairs += [(conv1_w, cw1), (conv2_w, cw2), (latent_hbm, x1.at[mine]), (emb_hbm, emb)]
+    pairs += [(conv1_w, cw1), (conv2_w, cw2), (latent_hbm, x1.at[mine])]
     loads = [pltpu.make_async_copy(a, b, lsem.at[i]) for i, (a, b) in enumerate(pairs)]
     L_T1, L_TP, L_Q, L_K, L_V, L_PW, L_OW, L_PO = loads[:8]
-    L_C1, L_C2, L_X, L_E = loads[8:]
-    for load in (L_X, L_E, L_T1, L_TP, L_C1, L_Q, L_K, L_V, L_PW, L_C2, L_OW, L_PO):
+    L_C1, L_C2, L_X = loads[8:]
+    for load in (L_X, L_T1, L_TP, L_C1, L_Q, L_K, L_V, L_PW, L_C2, L_OW, L_PO):
         load.start()
 
     def other(k, by, count):
@@ -265,13 +265,17 @@
     stats(x1[mine, :], 0)
     spread_w[...] = members(spread_w.shape, 1, own, 3)
 
+    half_width = FREQ // 2
+    place = lax.broadcasted_iota(jnp.int32, (16, FREQ), 1)
+    order = jnp.where(place < half_width, place, place - half_width).astype(F32)
+    angles = timestep[0].astype(F32) * jnp.exp(-math.log(10000.0) * order / half_width)
+    emb = jnp.where(place < half_width, jnp.cos(angles), jnp.sin(angles)).astype(BF16)
     pl.semaphore_wait(barrier, everyone - 1)
 
     share(0)
     gx[0].start()
     L_T1.wait()
-    L_E.wait()
-    hidden = silu(dot(emb[...], tw1[...]))
+    hidden = silu(dot(emb, tw1[...]))
     L_TP.wait()
     bias = dot_nt(tpj[...], silu(hidden).astype(BF16))
     gx[0].forward()
@@ -319,10 +323,10 @@
         beyond = jnp.where(2 * band < npatch - 1, rank, npatch - 1 - rank)
         return jnp.where(rank <= 2 * near, band + (1 - 2 * odd) * step, beyond)
 
+    stats(resnet, 2)
+    share(2)
     loop(1, npatch, lambda r: zrow(nearest(r), band).start())
     grow(band).start()
-    stats(resnet, 2)
-    share(2)
     grow(band).forward()
 
     def relay(rank):
@@ -366,7 +370,9 @@
         vals[source] = dot(vw[held, :], normed).astype(BF16)
         for h in range(nheads):
             part = slice(h * HEAD_DIM, (h + 1) * HEAD_DIM)
-            scores[source, h] = dot_tn(keys[part], query[part])
+            found = dot_tn(keys[part], query[part])
+            scores[source, h] = found
+            peaks[source, h] = jnp.max(found, axis=0, keepdims=True)
 
     projected, normed = project(band)
     proj[...] = projected
@@ -393,7 +399,7 @@
         part = slice(h * HEAD_DIM, (h + 1) * HEAD_DIM)
 
         def peak_of(b, peak):
-            return jnp.maximum(peak, jnp.max(scores[b, h], axis=0, keepdims=True))
+            return jnp.maximum(peak, peaks[b, h])
 
         def add(b, so_far):
             total, weighted = so_far
@@ -447,12 +453,6 @@
     nheads = -(-own // HEAD_DIM)
     nidx = nchan * nsub
     temb = time_w1.shape[0]
-    half_width = FREQ // 2
-    place = lax.broadcasted_iota(jnp.int32, (16, FREQ), 1)
-    first = place < half_width
-    order = jnp.where(first, place, place - half_width).astype(F32)
-    angles = timestep[0].astype(F32) * jnp.exp(-math.log(10000.0) * order / half_width)
-    emb = jnp.where(first, jnp.cos(angles), jnp.sin(angles)).astype(BF16)
     vmem = pl.BlockSpec(memory_space=pltpu.VMEM)
     hbm = pl.BlockSpec(memory_space=pl.ANY)
     dma = pltpu.SemaphoreType.DMA
@@ -461,10 +461,9 @@
     total = pl.pallas_call(
         functools.partial(kernel, npatch, nchan, nsub, own, nheads),
         out_shape=pltpu.VMEM((own, tokens), F32),
-        in_specs=[hbm] * 11,
+        in_specs=[hbm, pl.BlockSpec(memory_space=pltpu.SMEM)] + [hbm] * 9,
         out_specs=vmem,
         scratch_shapes=[
-            pltpu.VMEM((16, FREQ), BF16),
             pltpu.VMEM((FREQ, temb), BF16),
             pltpu.VMEM((own, temb), BF16),
             pltpu.VMEM((9, own, C), BF16),
@@ -487,10 +486,11 @@
             pltpu.VMEM((npatch, C, tokens), BF16),
             pltpu.VMEM((npatch, span, tokens), BF16),
             pltpu.VMEM((npatch, nheads, tokens, tokens), F32),
+            pltpu.VMEM((npatch, nheads, 1, tokens), F32),
             pltpu.VMEM((span, tokens), BF16),
             pltpu.VMEM((C, tokens), BF16),
             pltpu.VMEM((own, tokens), BF16),
-            dma((12,)),
+            dma((11,)),
             dma((ngather, nchan, nsub)),
             dma((ngather, nchan, nsub)),
             dma((3, npatch * nidx)),
@@ -504,7 +504,7 @@
             collective_id=0, has_side_effects=True, vmem_limit_bytes=60 * 1024 * 1024
         ),
     )(
-        latent, emb, time_w1.T, time_proj, conv1_w, conv2_w, proj_in_w, q_w, kv_w, out_w, proj_out_w
+        latent, timestep, time_w1.T, time_proj, conv1_w, conv2_w, proj_in_w, q_w, kv_w, out_w, proj_out_w
     )
     return total.astype(BF16)
 

time: 56.7 us -> 55.8 us (0.984)
  other arithmetic: 1.33 us -> 0.65 us
    convert_element_type x1 -> x0, other arithmetic: 0.68 us -> none  [local(): emb = jnp.where(first, jnp.cos(angles), jnp.sin(angles)).astype(BF16)]
where the time goes in v7:
time: 55.8 us; the launch traced here: 55.7 us
  Pallas kernels  54.4 us (97%)
  between operations  0.66 us (1%)
  other arithmetic  0.65 us (1%)
    pallas_call x1, Pallas kernels, local(): pl.pallas_call(functools.partial(kernel, npatch, nchan, nsub, own, nheads...  54.4 us

profile of v7, /device:TPU:1, one launch (start us, length us, event | category | flops | bytes accessed | tf_op | source)
XLA Modules:
  0.0 55.7 jit_solution(1789532473102990646)
XLA Ops:
  0.7 54.4 %shard_map.109 = f32[160,256]{1,0:T(8,128)S(1)} custom-call(bf16[160,256]{1,0:T(8,128)(2,1)} %latent_hbm.1, s32[1]{0:T(128)S(6)} %copy.12.timestep, bf16[320,1280]{1,0:T(8,128)(2,1)} %bitcast.1, bf16[160,1280]{1,0:T(8,128)(2,1)} %time_proj.1, bf16[9,160,640]{2,1,0:T(8,128)(2,1)} %conv1_w.1, bf16[9,160,640]{2,1,0:T(8,128)(2,1)} %conv2_w.1, ...), custom_call_target="tpu_custom_call" | custom-call | tf_op jit(solution)/shard_map/pallas_call | solution.py:461
  55.0 0.6 %convert_element_type.3 = bf16[160,256]{1,0:T(8,128)(2,1)} convert(f32[160,256]{1,0:T(8,128)S(1)} %shard_map.109) | non-fusion elementwise | flops 40960 | bytes 245760 | tf_op jit(solution)/shard_map/convert_element_type | solution.py:509

commit v8 on v7

--- a/solution.py
+++ b/solution.py
@@ -325,7 +325,7 @@
 
     stats(resnet, 2)
     share(2)
-    loop(1, npatch, lambda r: zrow(nearest(r), band).start())
+    loop(1, npatch, lambda r: zrow(nearest(npatch - r), band).start())
     grow(band).start()
     grow(band).forward()
 

time: 55.8 us -> 56.9 us (1.020)
  the two profiles are of different devices: /device:TPU:1 before, /device:TPU:21 now
where the time goes in v8:
time: 56.9 us; the launch traced here: 56.8 us
  Pallas kernels  55.4 us (97%)
  between operations  0.66 us (1%)
  other arithmetic  0.65 us (1%)
    pallas_call x1, Pallas kernels, local(): pl.pallas_call(functools.partial(kernel, npatch, nchan, nsub, own, nheads...  55.4 us

profile of v8, /device:TPU:21, one launch (start us, length us, event | category | flops | bytes accessed | tf_op | source)
XLA Modules:
  0.0 56.8 jit_solution(10271415973336286278)
XLA Ops:
  0.7 55.4 %shard_map.109 = f32[160,256]{1,0:T(8,128)S(1)} custom-call(bf16[160,256]{1,0:T(8,128)(2,1)} %latent_hbm.1, s32[1]{0:T(128)S(6)} %copy.12.timestep, bf16[320,1280]{1,0:T(8,128)(2,1)} %bitcast.1, bf16[160,1280]{1,0:T(8,128)(2,1)} %time_proj.1, bf16[9,160,640]{2,1,0:T(8,128)(2,1)} %conv1_w.1, bf16[9,160,640]{2,1,0:T(8,128)(2,1)} %conv2_w.1, ...), custom_call_target="tpu_custom_call" | custom-call | tf_op jit(solution)/shard_map/pallas_call | solution.py:461
  56.1 0.6 %convert_element_type.3 = bf16[160,256]{1,0:T(8,128)(2,1)} convert(f32[160,256]{1,0:T(8,128)S(1)} %shard_map.109) | non-fusion elementwise | flops 40960 | bytes 245760 | tf_op jit(solution)/shard_map/convert_element_type | solution.py:509
